TPU v7x, 256 devices: a whole 4x4x8 slice. The times are simulated.
256 devices in a mesh: dp: 32 (over x, y, core), tensor: 8 (over z).
Axes of the slice: x: 4, y: 4, z: 8, core: 2. Of those that a mesh axis runs over, the one named last changes fastest.
Arguments:
- patches: bfloat16 [32768, 1280], P('dp'), may hold values from -6 to 6
- vit_gain: float32 [1280], replicated, may hold values from 0.5 to 1.5
- fc_in: bfloat16 [1280, 5120], P(None, 'tensor'), may hold values from -0.15625 to 0.15625
- fc_out: bfloat16 [5120, 1280], P('tensor'), may hold values from -0.078125 to 0.078125
- merge_gain: float32 [1280], replicated, may hold values from 0.5 to 1.5
- merge_shift: float32 [1280], replicated, may hold values from -3 to 3
- merger: bfloat16 [5120, 8192], P('dp', 'tensor'), may hold values from -0.078125 to 0.078125
- counts: int32 [32, 32], replicated, may hold values from 0 to 16, as said below
- grad_packed: bfloat16 [16384, 8192], P('dp', 'tensor'), may hold values from -6 to 6
Outputs:
- visual: bfloat16 [16384, 8192], P('dp', 'tensor')
- grad_weight: float32 [5120, 8192], P('dp', 'tensor')
- grad_layer: float32 [32768, 1280], P(('dp', 'tensor'))
Inputs may be any that keep to these rules, and one draw needn't show every extreme that they name: counts[s, d] is the number of merged tokens that dp index s sends to dp index d, taken in order from s's 256 tokens; every row sums to 256 and holds the value 16 at least once.
All inputs are finite; a program needn't handle non-finite values.
Results may differ from a plain program's by a relative error of at most 0.023.
Values may be sent and summed in bfloat16 or wider, within the bound.
No kernel may reach another device: no remote copies, remote signals or barrier semaphores. Data moves between devices by JAX's collectives and lax.ppermute only.
A program may use at most 128 MiB of HBM per device.

v0:
```python
import math

import jax
import jax.numpy as jnp
from jax import lax
from jax.experimental import pallas as pl
from jax.experimental.pallas import tpu as pltpu
from jax.sharding import Mesh
from jax.sharding import PartitionSpec as P

epsilon = 1e-06
bf16 = jnp.bfloat16
f32 = jnp.float32
DP = ("x", "y", "c")
SWAP = [(0, 1), (1, 0)]
VMEM = 60 * 2**20


def vision_kernel(patches, gain, fc_in, fc_out, out):
    for r in range(0, patches.shape[0], 256):
        values = patches[r : r + 256, :].astype(f32)
        centered = values - jnp.mean(values, axis=-1, keepdims=True)
        variance = jnp.mean(centered * centered, axis=-1, keepdims=True)
        normed = (centered * lax.rsqrt(variance + epsilon) * gain[...]).astype(bf16)
        hidden = jnp.dot(normed, fc_in[...], preferred_element_type=f32)
        hidden = (hidden * jax.nn.sigmoid(1.702 * hidden)).astype(bf16)
        term = jnp.dot(hidden, fc_out[...], preferred_element_type=f32)
        out[r : r + 256, :] = term.astype(bf16)


def vision(patches, gain, fc_in, fc_out):
    rows, width = patches.shape
    tile = pl.BlockSpec((512, width), lambda i: (i, 0))
    return pl.pallas_call(
        vision_kernel,
        out_shape=jax.ShapeDtypeStruct((rows, width), bf16),
        grid=(rows // 512,),
        in_specs=[tile, pl.BlockSpec((width,), lambda i: (0,))]
        + [pl.BlockSpec(a.shape, lambda i: (0, 0)) for a in (fc_in, fc_out)],
        out_specs=tile,
        compiler_params=pltpu.CompilerParams(vmem_limit_bytes=VMEM),
        cost_estimate=pl.CostEstimate(flops=4 * rows * width * 640, bytes_accessed=9 * 2**20, transcendentals=rows * 640),
        name="vision",
    )(patches, gain, fc_in, fc_out)


def norm_kernel(z, patches, summed, gain, shift, tokens, normal, inverse, held):
    layer_out = patches[...].astype(f32) + summed[...].astype(f32)
    centered = layer_out - jnp.mean(layer_out, axis=-1, keepdims=True)
    scale = lax.rsqrt(jnp.mean(centered * centered, axis=-1, keepdims=True) + epsilon)
    normal[...] = centered * scale
    inverse[...] = jnp.broadcast_to(scale, inverse.shape)
    held[...] = (normal[...] * gain[...] + shift[...]).reshape(held.shape)
    for j in range(4):
        tokens[:, 1280 * j : 1280 * (j + 1)] = held[:, j, :].astype(bf16)


def norm(z, patches, summed, gain, shift):
    fixed = lambda i, z: (0, 0)
    row = pl.BlockSpec((1280,), lambda i, z: (0,))
    return pl.pallas_call(
        norm_kernel,
        out_shape=[
            jax.ShapeDtypeStruct((32, 5120), bf16),
            jax.ShapeDtypeStruct((128, 1280), f32),
            jax.ShapeDtypeStruct((128, 128), f32),
        ],
        grid_spec=pltpu.PrefetchScalarGridSpec(
            num_scalar_prefetch=1,
            grid=(1,),
            in_specs=[
                pl.BlockSpec((128, 1280), lambda i, z: (z[0], 0)),
                pl.BlockSpec((128, 1280), fixed),
                row,
                row,
            ],
            out_specs=[
                pl.BlockSpec((32, 5120), fixed),
                pl.BlockSpec((128, 1280), fixed),
                pl.BlockSpec((128, 128), fixed),
            ],
            scratch_shapes=[pltpu.VMEM((32, 4, 1280), f32)],
        ),
        compiler_params=pltpu.CompilerParams(vmem_limit_bytes=VMEM),
        name="norm",
    )(z, patches, summed, gain, shift)


def grad_kernel(grads, normal, inverse, gain, out, held):
    for j in range(4):
        held[:, j, :] = grads[:, 1280 * j : 1280 * (j + 1)].astype(f32)
    scaled = held[...].reshape(128, 1280) * gain[...]
    unit = normal[...]
    inner = jnp.mean(scaled * unit, axis=-1, keepdims=True)
    out[...] = inverse[:, :1] * (scaled - jnp.mean(scaled, axis=-1, keepdims=True) - unit * inner)


def layer_grad(grads, normal, inverse, gain):
    return pl.pallas_call(
        grad_kernel,
        out_shape=jax.ShapeDtypeStruct((128, 1280), f32),
        scratch_shapes=[pltpu.VMEM((32, 4, 1280), f32)],
        compiler_params=pltpu.CompilerParams(vmem_limit_bytes=VMEM),
        name="layer_grad",
    )(grads, normal, inverse, gain)


def exclusive_sum(values):
    return jnp.cumsum(values) - values


def position(x, y, c):
    return (x * 4 + y) * 2 + c


def mask(c, turn):
    return 1 + 2 * ((c + turn) % 2)


def swap(array, axis, turn):
    pairs = []
    for x in range(4):
        for y in range(4):
            for c in range(2):
                m = mask(c, turn)
                to = position(x ^ m, y, c) if axis == "x" else position(x, y ^ m, c)
                pairs.append((position(x, y, c), to))
    return lax.ppermute(array, DP, pairs)


def places():
    c = lax.axis_index("c")
    return {"x": lax.axis_index("x"), "y": lax.axis_index("y")}, mask(c, 0), mask(c, 1)


def pick(array, index):
    return lax.dynamic_index_in_dim(array, index, 0, keepdims=False)


def gather_lines(block):
    place, near, far = places()
    lines = []
    for i, axis in enumerate("yx"):
        at = place[axis]
        mine = block[:, 256 * i : 256 * (i + 1)]
        one = swap(mine, axis, 0)
        two = swap(jnp.stack([mine, one]), axis, 1)
        line = jnp.broadcast_to(mine, (4, 320, 256))
        for index, part in ((at ^ near, one), (at ^ far, two[0]), (at ^ 2, two[1])):
            line = lax.dynamic_update_index_in_dim(line, part, index, 0)
        lines.append(line)
    return lines


def gather_chips(lines, after):
    place, near, far = places()
    ones = [swap(line, axis, 0) for line, axis in zip(lines, "xy")]
    lines, ones, after = lax.optimization_barrier((lines, ones, after))
    whole = jnp.zeros((4, 4, 320, 512), bf16)
    for i, axis in enumerate("xy"):
        at = place[axis]
        two = swap(jnp.stack([lines[i], ones[i]]), axis, 1)
        for index, part in ((at, lines[i]), (at ^ near, ones[i]), (at ^ far, two[0]), (at ^ 2, two[1])):
            if axis == "x":
                whole = lax.dynamic_update_slice(whole, part[None], (index, 0, 0, 256 * i))
            else:
                whole = lax.dynamic_update_slice(whole, part[:, None], (0, index, 0, 256 * i))
    return whole.reshape(5120, 512), after


def weight_kernel(order, tokens, grads, give_x, keep_x, give_y, keep_y, held):
    total = lax.dot_general(
        tokens[...], grads[...], (((0,), (0,)), ((), ())), preferred_element_type=f32
    ).astype(bf16)

    @pl.when(pl.program_id(0) < 2)
    def _():
        give_x[0] = total[:, :256]

    @pl.when(pl.program_id(0) >= 2)
    def _():
        keep_x[0] = total[:, :256]

    held[...] = total[:, 256:]

    def rows(m):
        return held[pl.ds(pl.multiple_of(order[4 + m] * 320, 64), 320), :]

    for m in range(2):
        give_y[m, 0] = rows(m)
        keep_y[m, 0] = rows(2 + m)


def weight_blocks(tokens, grads, later):
    place, near, far = places()
    masks = jnp.stack([far, 2, 0, near])
    order = jnp.concatenate([place["x"] ^ masks, place["y"] ^ masks]).astype(jnp.int32)
    flat = jax.ShapeDtypeStruct((2, 1280, 256), bf16)
    deep = jax.ShapeDtypeStruct((2, 4, 320, 256), bf16)
    give_x, keep_x, give_y, keep_y = pl.pallas_call(
        weight_kernel,
        out_shape=[flat, flat, deep, deep],
        grid_spec=pltpu.PrefetchScalarGridSpec(
            num_scalar_prefetch=1,
            grid=(4,),
            in_specs=[
                pl.BlockSpec((512, 1280), lambda k, o: (0, o[k])),
                pl.BlockSpec((512, 512), lambda k, o: (0, 0)),
            ],
            out_specs=[
                pl.BlockSpec((1, 1280, 256), lambda k, o: (jnp.minimum(k, 1), 0, 0)),
                pl.BlockSpec((1, 1280, 256), lambda k, o: (jnp.maximum(k - 2, 0), 0, 0)),
            ]
            + [pl.BlockSpec((2, 1, 320, 256), lambda k, o: (0, o[k], 0, 0))] * 2,
            scratch_shapes=[pltpu.VMEM((1280, 256), bf16)],
        ),
        compiler_params=pltpu.CompilerParams(vmem_limit_bytes=VMEM),
        cost_estimate=pl.CostEstimate(flops=16 * 512 * 1280 * 256, bytes_accessed=11 * 2**20, transcendentals=0),
        name="weight_product",
    )(order, tokens, grads)
    give_x, later = lax.optimization_barrier((give_x, later))
    along_x = [p.reshape(2, 4, 320, 256) for p in (give_x, keep_x)]
    return along_x, (give_y, keep_y), later


def scatter_chips(blocks, later):
    came = [swap(give, axis, 1) for (give, _), axis in zip(blocks, "xy")]
    passed = [
        (c[1].astype(f32) + keep[1].astype(f32)).astype(bf16) for c, (_, keep) in zip(came, blocks)
    ]
    passed, later = lax.optimization_barrier((passed, later))
    last = [swap(p, axis, 0) for p, axis in zip(passed, "xy")]
    sums = [
        (c[0].astype(f32) + keep[0].astype(f32) + end.astype(f32)).astype(bf16)
        for c, (_, keep), end in zip(came, blocks, last)
    ]
    return sums, later


def exchange_chips(running, earlier):
    place, near, far = places()
    sums = []
    for line, axis in zip(running, "yx"):
        at = place[axis]
        came = swap(jnp.stack([pick(line, at ^ far), pick(line, at ^ 2)]), axis, 1)
        passed = (came[1].astype(f32) + pick(line, at ^ near).astype(f32)).astype(bf16)
        end = swap(passed, axis, 0)
        if axis == "x":
            end, earlier = lax.optimization_barrier((end, earlier))
        sums.append(came[0].astype(f32) + pick(line, at).astype(f32) + end.astype(f32))
    return sums, earlier


def body(patches, vit_gain, fc_in, fc_out, merge_gain, merge_shift, merger, counts, grad_packed):
    core = lax.axis_index("c")
    chip = lax.axis_index("x") * 4 + lax.axis_index("y")
    me = chip * 2 + core
    z = lax.axis_index("z")

    halves = merger.reshape(160, 2, 512)
    kept = lax.dynamic_index_in_dim(halves, core, 1, keepdims=False)
    given = lax.dynamic_index_in_dim(halves, 1 - core, 1, keepdims=False)
    got = lax.ppermute(given, "c", SWAP)
    both = jnp.where(core == 0, jnp.concatenate([kept, got]), jnp.concatenate([got, kept]))
    lines = gather_lines(both)

    summed = lax.psum_scatter(
        vision(patches, vit_gain, fc_in, fc_out), "z", scatter_dimension=0, tiled=True
    )

    slot = jnp.arange(16, dtype=jnp.int32)
    recv_counts = lax.dynamic_index_in_dim(counts, me, 1, keepdims=False)
    recv_start = exclusive_sum(recv_counts)
    packed_row = jnp.where(
        slot[None, :] < recv_counts[:, None], recv_start[:, None] + slot[None, :], -1
    ).reshape(512)
    pack = (packed_row[:, None] == jnp.arange(512, dtype=jnp.int32)[None, :]).astype(bf16)
    send_counts = lax.dynamic_slice_in_dim(counts, chip * 2, 2, 0)
    send_start = jnp.cumsum(send_counts, axis=1) - send_counts
    base = 256 * jnp.arange(2, dtype=jnp.int32)
    first = send_start.T[:, :, None] + slot + base[None, :, None]
    token = jnp.where(slot < send_counts.T[:, :, None], first, -1).reshape(1024)
    route = (jnp.arange(512, dtype=jnp.int32)[:, None] == token[None, :]).astype(bf16)

    returning = jnp.stack(
        [
            jnp.dot(pack, grad_packed[:, :512], preferred_element_type=f32).astype(bf16).reshape(16, 32, 512),
            jnp.dot(pack, grad_packed[:, 512:], preferred_element_type=f32).astype(bf16).reshape(16, 32, 512),
        ],
        axis=1,
    ).reshape(32, 32, 512)
    arrived = lax.all_to_all(returning, DP, split_axis=0, concat_axis=0, tiled=True)
    summed, arrived = lax.optimization_barrier((summed, arrived))
    token_grads = jnp.dot(
        route, arrived.reshape(1024, 512), preferred_element_type=f32
    ).astype(bf16)

    normed_mine, normal, inverse = norm(
        z[None], patches, summed, merge_gain, merge_shift
    )
    weight, normed_mine = gather_chips(lines, normed_mine)
    merged = lax.all_gather(normed_mine, ("c", "z"), axis=0, tiled=True)

    def back(grads):
        return lax.dot_general(
            grads, weight, (((1,), (1,)), ((), ())), preferred_element_type=f32
        ).astype(bf16)

    by_core = token_grads.reshape(2, 256, 512)
    given = lax.ppermute(back(pick(by_core, 1 - core)), "c", SWAP)
    chip_grads = (back(pick(by_core, core)).astype(f32) + given.astype(f32)).astype(bf16)

    projected = jnp.dot(merged, weight, preferred_element_type=f32).astype(bf16)
    outgoing = lax.dot_general(
        route, projected, (((0,), (0,)), ((), ())), preferred_element_type=f32
    ).astype(bf16)

    first_x, first_y, chip_grads = weight_blocks(merged, token_grads, chip_grads)
    running, outgoing = scatter_chips((first_x, first_y), outgoing)
    incoming = lax.all_to_all(
        outgoing.reshape(32, 32, 512), DP, split_axis=0, concat_axis=0, tiled=True
    ).reshape(16, 2, 512 // 16, 512)
    visual = jnp.concatenate(
        [
            lax.dot_general(
                pack,
                incoming[:, h].reshape(512, 512),
                (((0,), (0,)), ((), ())),
                preferred_element_type=f32,
            ).astype(bf16)
            for h in range(2)
        ],
        axis=1,
    )

    merged_grads = lax.psum_scatter(chip_grads, "z", scatter_dimension=0, tiled=True)
    grad_layer = layer_grad(merged_grads, normal, inverse, merge_gain)

    sums, grad_layer = exchange_chips(running, grad_layer)
    chip_rows = jnp.concatenate(sums, axis=1).reshape(2, 160, 512) * (1.0 / math.sqrt(8192))
    mine = pick(chip_rows, core)
    other = lax.ppermute(
        pick(chip_rows, 1 - core), "c", SWAP
    )
    grad_weight = jnp.where(
        core == 0,
        jnp.concatenate([mine, other], axis=1),
        jnp.concatenate([other, mine], axis=1),
    )
    return (visual, grad_weight, grad_layer)


def solution(mesh):
    grid = Mesh(mesh.devices.reshape(4, 4, 2, 8), ("x", "y", "c", "z"))
    in_specs = (
        P(DP, None),
        P(),
        P(None, "z"),
        P("z", None),
        P(),
        P(),
        P(DP, "z"),
        P(),
        P(DP, "z"),
    )
    out_specs = (P(DP, "z"), P(DP, "z"), P((*DP, "z"), None))
    return jax.shard_map(body, mesh=grid, in_specs=in_specs, out_specs=out_specs, check_vma=False)
```

profile of v0, /device:TPU:1, one launch (start us, length us, event | category | flops | bytes accessed | tf_op | source)
XLA Modules:
  0.0 192.6 jit_solution(5612648280664868337)
XLA Ops:
  7.2 9.0 %vision.1 = bf16[1024,1280]{1,0:T(8,128)(2,1)} custom-call(bf16[1024,1280]{1,0:T(8,128)(2,1)} %patches.3, f32[1280]{0:T(1024)} %gain.3, bf16[1280,640]{1,0:T(8,128)(2,1)} %fc_in.1, bf16[640,1280]{1,0:T(8,128)(2,1)} %fc_out.1), custom_call_target="tpu_custom_call" | custom-call | flops 3355443200 | bytes 9437184 | tf_op jit(solution)/shard_map/vision/pallas_call | solution.py:34
  18.1 3.3 %collective-permute-start = (bf16[160,512]{1,0:T(8,128)(2,1)S(1)}, bf16[160,512]{1,0:T(8,128)(2,1)S(1)}, u32[]{:S(2)}, u32[]{:S(2)}) collective-permute-start(bf16[160,512]{1,0:T(8,128)(2,1)S(1)} %bitcast.127), channel_id=1, source_target_pairs={{0,8},{8,0},{1,9},{9,1},{2,10},{10,2},{3,11},{11,3},{4,12},{12,4},... | collective-permute-start | bytes 491528 | tf_op jit(solution)/shard_map/ppermute | solution.py:263
  24.0 2.8 %collective-permute-start.1 = (bf16[320,256]{1,0:T(8,128)(2,1)S(1)}, bf16[320,256]{1,0:T(8,128)(2,1)S(1)}, u32[]{:S(2)}, u32[]{:S(2)}) collective-permute-start(bf16[320,256]{1,0:T(8,128)(2,1)S(1)} %get-tuple-element.71), channel_id=1, source_target_pairs={{0,16},{8,56},{16,0},{24,40},{32,48},{40,24},{48,32},{56,8},{64,80... | collective-permute-start | bytes 491528 | tf_op jit(solution)/shard_map/ppermute | solution.py:128
  27.8 4.8 %all-to-all-start = ((bf16[32,32,512]{2,1,0:T(8,128)(2,1)}), bf16[32,32,512]{2,1,0:T(8,128)(2,1)}, u32[]{:S(2)}, u32[]{:S(2)}) async-start(bf16[32,32,512]{2,1,0:T(8,128)(2,1)} %bitcast.11), calls=%async_computation.1 | async-start | bytes 2097152 | tf_op jit(solution)/shard_map/all_to_all | solution.py:292
  35.7 14.4 %collective-permute-done.4 = bf16[2,320,256]{2,1,0:T(8,128)(2,1)S(1)} collective-permute-done((bf16[2,320,256]{2,1,0:T(8,128)(2,1)S(1)}, bf16[2,320,256]{2,1,0:T(8,128)(2,1)S(1)}, u32[]{:S(2)}, u32[]{:S(2)}) %collective-permute-start.4) | collective-permute-done | bytes 327712 | tf_op jit(solution)/shard_map/ppermute | solution.py:128
  50.2 2.5 %collective-permute-start.6 = (bf16[4,320,256]{2,1,0:T(8,128)(2,1)S(1)}, bf16[4,320,256]{2,1,0:T(8,128)(2,1)S(1)}, u32[]{:S(2)}, u32[]{:S(2)}) collective-permute-start(bf16[4,320,256]{2,1,0:T(8,128)(2,1)S(1)} %slice_dynamic-update-slice_fusion.2), channel_id=1, source_target_pairs={{0,16},{8,56},{16,0},{24,40},{32,48},{40,24},{48,32},{56,8},{64,80... | collective-permute-start | bytes 1966088 | tf_op jit(solution)/shard_map/ppermute | solution.py:128
  54.6 6.1 %reduce-scatter.3.cloned.1.call-done.summed = bf16[128,1280]{1,0:T(8,128)(2,1)} async-done(((bf16[1024,1280]{1,0:T(8,128)(2,1)}), bf16[128,1280]{1,0:T(8,128)(2,1)}) %reduce-scatter.3.cloned.1.call-update) | async-done | bytes 327696 | tf_op jit(solution)/shard_map/reduce_scatter | solution.py:267
  60.7 2.9 %norm.1 = (bf16[32,5120]{1,0:T(8,128)(2,1)}, f32[128,1280]{1,0:T(8,128)}, f32[128,128]{1,0:T(8,128)}) custom-call(s32[1]{0:T(128)} %bitcast.6.z, bf16[1024,1280]{1,0:T(8,128)(2,1)} %patches.3, bf16[128,1280]{1,0:T(8,128)(2,1)} %reduce-scatter.3.cloned.1.call-done.summed, f32[1280]{0:T(1024)} %gain.5, f32[1280]{0:T(1024)} %shift.1), custom_call_target="tpu_custom_call" | custom-call | tf_op jit(solution)/shard_map/norm/pallas_call | solution.py:61
  70.7 11.5 %collective-permute-done.7 = bf16[2,4,320,256]{3,2,1,0:T(8,128)(2,1)} collective-permute-done((bf16[2,4,320,256]{3,2,1,0:T(8,128)(2,1)}, bf16[2,4,320,256]{3,2,1,0:T(8,128)(2,1)}, u32[]{:S(2)}, u32[]{:S(2)}) %collective-permute-start.7) | collective-permute-done | bytes 1310752 | tf_op jit(solution)/shard_map/ppermute | solution.py:128
  86.4 7.0 %collective-permute-start.9 = (bf16[256,5120]{1,0:T(8,128)(2,1)S(1)}, bf16[256,5120]{1,0:T(8,128)(2,1)S(1)}, u32[]{:S(2)}, u32[]{:S(2)}) collective-permute-start(bf16[256,5120]{1,0:T(8,128)(2,1)S(1)} %convolution_convert_fusion), channel_id=1, source_target_pairs={{0,8},{8,0},{1,9},{9,1},{2,10},{10,2},{3,11},{11,3},{4,12},{12,4},... | collective-permute-start | bytes 7864328 | tf_op jit(solution)/shard_map/ppermute | solution.py:310
  94.1 4.3 %collective-permute-done.9 = bf16[256,5120]{1,0:T(8,128)(2,1)S(1)} collective-permute-done((bf16[256,5120]{1,0:T(8,128)(2,1)S(1)}, bf16[256,5120]{1,0:T(8,128)(2,1)S(1)}, u32[]{:S(2)}, u32[]{:S(2)}) %collective-permute-start.9) | collective-permute-done | bytes 2621472 | tf_op jit(solution)/shard_map/ppermute | solution.py:310
  98.4 3.1 %fusion.2 = bf16[256,5120]{1,0:T(8,128)(2,1)} fusion(bf16[5120,512]{1,0:T(8,128)(2,1)S(1)} %bitcast.107, bf16[256,5120]{1,0:T(8,128)(2,1)S(1)} %collective-permute-done.9, bf16[2,256,512]{2,1,0:T(8,128)(2,1)S(1)} %bitcast.122, s32[]{:T(128)S(6)} %select_n.127), kind=kOutput, calls=%fused_computation.4 | convolution fusion | flops 1348730880 | bytes 10747908 | tf_op jit(solution)/shard_map/dot_general | solution.py:305
  101.5 9.1 %all-gather.2.cloned.1.call-done.tokens = bf16[512,5120]{1,0:T(8,128)(2,1)} async-done(((bf16[32,5120]{1,0:T(8,128)(2,1)}), bf16[512,5120]{1,0:T(8,128)(2,1)}) %all-gather.2.cloned.1.call-update) | async-done | bytes 5242896 | tf_op jit(solution)/shard_map/all_gather | solution.py:302
  110.6 8.3 %weight_product.1 = (bf16[2,1280,256]{2,1,0:T(8,128)(2,1)}, bf16[2,1280,256]{2,1,0:T(8,128)(2,1)}, bf16[2,4,320,256]{3,2,1,0:T(8,128)(2,1)}, bf16[2,4,320,256]{3,2,1,0:T(8,128)(2,1)}) custom-call(s32[8]{0:T(128)} %pad_add_fusion.1.order, bf16[512,5120]{1,0:T(8,128)(2,1)} %all-gather.2.cloned.1.call-done.tokens, bf16[512,512]{1,0:T(8,128)(2,1)} %copy-done.5), custom_call_target="tpu_custom_call" | custom-call | flops 2684354560 | bytes 11534336 | tf_op jit(solution)/shard_map/weight_product/pallas_call | solution.py:200
  121.6 8.5 %fusion.5 = bf16[1024,512]{1,0:T(8,128)(2,1)} fusion(s32[1024]{0:T(1024)S(1)} %select_n.138, bf16[512,5120]{1,0:T(8,128)(2,1)} %all-gather.2.cloned.1.call-done.tokens, bf16[5120,512]{1,0:T(8,128)(2,1)} %bitcast.108), kind=kOutput, calls=%fused_computation.8 | convolution fusion | flops 3222536192 | bytes 11538432 | tf_op jit(solution)/shard_map/dot_general | solution.py:314
  130.1 5.8 %collective-permute-done.10 = bf16[2,4,320,256]{3,2,1,0:T(8,128)(2,1)} collective-permute-done((bf16[2,4,320,256]{3,2,1,0:T(8,128)(2,1)}, bf16[2,4,320,256]{3,2,1,0:T(8,128)(2,1)}, u32[]{:S(2)}, u32[]{:S(2)}) %collective-permute-start.10) | collective-permute-done | bytes 1310752 | tf_op jit(solution)/shard_map/ppermute | solution.py:128
  135.9 2.1 %fusion.8 = bf16[4,320,256]{2,1,0:T(8,128)(2,1)} fusion(bf16[4,320,256]{2,1,0:T(8,128)(2,1)S(1)} %bitcast.115, bf16[2,4,320,256]{3,2,1,0:T(8,128)(2,1)} %collective-permute-done.10), kind=kLoop, calls=%fused_computation.15 | loop fusion | flops 1310720 | bytes 1966080 | tf_op jit(solution)/shard_map/convert_element_type | solution.py:229
  138.0 2.1 %fusion.13 = bf16[4,320,256]{2,1,0:T(8,128)(2,1)} fusion(bf16[2,4,320,256]{3,2,1,0:T(8,128)(2,1)} %collective-permute-done.11, bf16[2,4,320,256]{3,2,1,0:T(8,128)(2,1)S(1)} %copy-done.1), kind=kLoop, calls=%fused_computation.30 | loop fusion | flops 1310720 | bytes 1966080 | tf_op jit(solution)/shard_map/convert_element_type | solution.py:229
  140.1 2.4 %collective-permute-start.12 = (bf16[4,320,256]{2,1,0:T(8,128)(2,1)}, bf16[4,320,256]{2,1,0:T(8,128)(2,1)S(1)}, u32[]{:S(2)}, u32[]{:S(2)}) collective-permute-start(bf16[4,320,256]{2,1,0:T(8,128)(2,1)} %fusion.8), channel_id=1, source_target_pairs={{0,64},{8,200},{16,80},{24,216},{32,96},{40,232},{48,112},{56,248}... | collective-permute-start | bytes 1966088 | tf_op jit(solution)/shard_map/ppermute | solution.py:128
  142.5 2.6 %collective-permute-start.15 = (bf16[4,320,256]{2,1,0:T(8,128)(2,1)}, bf16[4,320,256]{2,1,0:T(8,128)(2,1)S(1)}, u32[]{:S(2)}, u32[]{:S(2)}) collective-permute-start(bf16[4,320,256]{2,1,0:T(8,128)(2,1)} %fusion.13), channel_id=1, source_target_pairs={{0,16},{8,56},{16,0},{24,40},{32,48},{40,24},{48,32},{56,8},{64,80... | collective-permute-start | bytes 1966088 | tf_op jit(solution)/shard_map/ppermute | solution.py:128
  145.1 6.7 %all-to-all-start.1 = ((bf16[32,32,512]{2,1,0:T(8,128)(2,1)}), bf16[32,32,512]{2,1,0:T(8,128)(2,1)S(1)}, u32[]{:S(2)}, u32[]{:S(2)}) async-start(bf16[32,32,512]{2,1,0:T(8,128)(2,1)} %bitcast.117), calls=%async_computation.2 | async-start | bytes 2097152 | tf_op jit(solution)/shard_map/all_to_all | solution.py:320
  158.6 10.8 %collective-permute-done.13 = bf16[2,320,256]{2,1,0:T(8,128)(2,1)S(1)} collective-permute-done((bf16[2,320,256]{2,1,0:T(8,128)(2,1)S(1)}, bf16[2,320,256]{2,1,0:T(8,128)(2,1)S(1)}, u32[]{:S(2)}, u32[]{:S(2)}) %collective-permute-start.13) | collective-permute-done | bytes 327712 | tf_op jit(solution)/shard_map/ppermute | solution.py:128
  172.7 2.2 %collective-permute-start.17 = (bf16[320,256]{1,0:T(8,128)(2,1)}, bf16[320,256]{1,0:T(8,128)(2,1)}, u32[]{:S(2)}, u32[]{:S(2)}) collective-permute-start(bf16[320,256]{1,0:T(8,128)(2,1)} %fusion.27), channel_id=1, source_target_pairs={{0,64},{8,200},{16,80},{24,216},{32,96},{40,232},{48,112},{56,248}... | collective-permute-start | bytes 491528 | tf_op jit(solution)/shard_map/ppermute | solution.py:128
  176.8 2.6 %layer_grad.1 = f32[128,1280]{1,0:T(8,128)} custom-call(bf16[32,5120]{1,0:T(8,128)(2,1)} %reduce-scatter.5.cloned.1.call-done.grads, f32[128,1280]{1,0:T(8,128)} %get-tuple-element.41.normal, f32[128,128]{1,0:T(8,128)} %get-tuple-element.42.inverse, f32[1280]{0:T(1024)} %gain.5), custom_call_target="tpu_custom_call" | custom-call | tf_op jit(solution)/shard_map/layer_grad/pallas_call | solution.py:99
  (129 shorter events, 43.5 us)
Async XLA Ops:
  7.2 53.5 %reduce-scatter.3.cloned.1.call-start = ((), (), s32[]{:S(2)}) async-start(), calls=%async_computation.4 | async-start | bytes 2949120 | tf_op jit(solution)/shard_map/reduce_scatter | solution.py:267
  18.1 4.4 %collective-permute-start = (bf16[160,512]{1,0:T(8,128)(2,1)S(1)}, bf16[160,512]{1,0:T(8,128)(2,1)S(1)}, u32[]{:S(2)}, u32[]{:S(2)}) collective-permute-start(bf16[160,512]{1,0:T(8,128)(2,1)S(1)} %bitcast.127), channel_id=1, source_target_pairs={{0,8},{8,0},{1,9},{9,1},{2,10},{10,2},{3,11},{11,3},{4,12},{12,4},... | collective-permute-start | bytes 491528 | tf_op jit(solution)/shard_map/ppermute | solution.py:263
  22.6 10.1 %collective-permute-start.3 = (bf16[320,256]{1,0:T(8,128)(2,1)S(1)}, bf16[320,256]{1,0:T(8,128)(2,1)S(1)}, u32[]{:S(2)}, u32[]{:S(2)}) collective-permute-start(bf16[320,256]{1,0:T(8,128)(2,1)S(1)} %get-tuple-element.70), channel_id=1, source_target_pairs={{0,64},{8,200},{16,80},{24,216},{32,96},{40,232},{48,112},{56,248}... | collective-permute-start | bytes 491528 | tf_op jit(solution)/shard_map/ppermute | solution.py:128
  24.0 10.3 %collective-permute-start.1 = (bf16[320,256]{1,0:T(8,128)(2,1)S(1)}, bf16[320,256]{1,0:T(8,128)(2,1)S(1)}, u32[]{:S(2)}, u32[]{:S(2)}) collective-permute-start(bf16[320,256]{1,0:T(8,128)(2,1)S(1)} %get-tuple-element.71), channel_id=1, source_target_pairs={{0,16},{8,56},{16,0},{24,40},{32,48},{40,24},{48,32},{56,8},{64,80... | collective-permute-start | bytes 491528 | tf_op jit(solution)/shard_map/ppermute | solution.py:128
  27.8 26.8 %all-to-all-start = ((bf16[32,32,512]{2,1,0:T(8,128)(2,1)}), bf16[32,32,512]{2,1,0:T(8,128)(2,1)}, u32[]{:S(2)}, u32[]{:S(2)}) async-start(bf16[32,32,512]{2,1,0:T(8,128)(2,1)} %bitcast.11), calls=%async_computation.1 | async-start | bytes 2097152 | tf_op jit(solution)/shard_map/all_to_all | solution.py:292
  32.6 78.0 %all-gather.2.cloned.1.call-start = ((), (), s32[]{:S(2)}) async-start(), calls=%async_computation.5 | async-start | bytes 5570560 | tf_op jit(solution)/shard_map/all_gather | solution.py:302
  32.8 17.4 %collective-permute-start.4 = (bf16[2,320,256]{2,1,0:T(8,128)(2,1)S(1)}, bf16[2,320,256]{2,1,0:T(8,128)(2,1)S(1)}, u32[]{:S(2)}, u32[]{:S(2)}) collective-permute-start(bf16[2,320,256]{2,1,0:T(8,128)(2,1)S(1)} %pad_maximum_fusion.5), channel_id=1, source_target_pairs={{0,192},{8,72},{16,208},{24,88},{32,224},{40,104},{48,240},{56,120... | collective-permute-start | bytes 983048 | tf_op jit(solution)/shard_map/ppermute | solution.py:128
  34.3 18.4 %collective-permute-start.2 = (bf16[2,320,256]{2,1,0:T(8,128)(2,1)S(1)}, bf16[2,320,256]{2,1,0:T(8,128)(2,1)S(1)}, u32[]{:S(2)}, u32[]{:S(2)}) collective-permute-start(bf16[2,320,256]{2,1,0:T(8,128)(2,1)S(1)} %pad_maximum_fusion.4), channel_id=1, source_target_pairs={{0,48},{8,24},{16,32},{24,8},{32,16},{40,56},{48,0},{56,40},{64,11... | collective-permute-start | bytes 983048 | tf_op jit(solution)/shard_map/ppermute | solution.py:128
  50.2 13.4 %collective-permute-start.6 = (bf16[4,320,256]{2,1,0:T(8,128)(2,1)S(1)}, bf16[4,320,256]{2,1,0:T(8,128)(2,1)S(1)}, u32[]{:S(2)}, u32[]{:S(2)}) collective-permute-start(bf16[4,320,256]{2,1,0:T(8,128)(2,1)S(1)} %slice_dynamic-update-slice_fusion.2), channel_id=1, source_target_pairs={{0,16},{8,56},{16,0},{24,40},{32,48},{40,24},{48,32},{56,8},{64,80... | collective-permute-start | bytes 1966088 | tf_op jit(solution)/shard_map/ppermute | solution.py:128
  52.7 10.9 %collective-permute-start.5 = (bf16[4,320,256]{2,1,0:T(8,128)(2,1)S(1)}, bf16[4,320,256]{2,1,0:T(8,128)(2,1)S(1)}, u32[]{:S(2)}, u32[]{:S(2)}) collective-permute-start(bf16[4,320,256]{2,1,0:T(8,128)(2,1)S(1)} %slice_dynamic-update-slice_fusion.4), channel_id=1, source_target_pairs={{0,64},{8,200},{16,80},{24,216},{32,96},{40,232},{48,112},{56,248}... | collective-permute-start | bytes 1966088 | tf_op jit(solution)/shard_map/ppermute | solution.py:128
  63.7 113.1 %reduce-scatter.5.cloned.1.call-start = ((), (), s32[]{:S(2)}) async-start(), calls=%async_computation.6 | async-start | bytes 2949120 | tf_op jit(solution)/shard_map/reduce_scatter | solution.py:336
  65.1 17.1 %collective-permute-start.7 = (bf16[2,4,320,256]{3,2,1,0:T(8,128)(2,1)}, bf16[2,4,320,256]{3,2,1,0:T(8,128)(2,1)}, u32[]{:S(2)}, u32[]{:S(2)}) collective-permute-start(bf16[2,4,320,256]{3,2,1,0:T(8,128)(2,1)} %pad_maximum_fusion), channel_id=1, source_target_pairs={{0,192},{8,72},{16,208},{24,88},{32,224},{40,104},{48,240},{56,120... | collective-permute-start | bytes 3932168 | tf_op jit(solution)/shard_map/ppermute | solution.py:128
  66.9 17.8 %collective-permute-start.8 = (bf16[2,4,320,256]{3,2,1,0:T(8,128)(2,1)S(1)}, bf16[2,4,320,256]{3,2,1,0:T(8,128)(2,1)S(1)}, u32[]{:S(2)}, u32[]{:S(2)}) collective-permute-start(bf16[2,4,320,256]{3,2,1,0:T(8,128)(2,1)S(1)} %pad_maximum_fusion.1), channel_id=1, source_target_pairs={{0,48},{8,24},{16,32},{24,8},{32,16},{40,56},{48,0},{56,40},{64,11... | collective-permute-start | bytes 3932168 | tf_op jit(solution)/shard_map/ppermute | solution.py:128
  86.4 12.0 %collective-permute-start.9 = (bf16[256,5120]{1,0:T(8,128)(2,1)S(1)}, bf16[256,5120]{1,0:T(8,128)(2,1)S(1)}, u32[]{:S(2)}, u32[]{:S(2)}) collective-permute-start(bf16[256,5120]{1,0:T(8,128)(2,1)S(1)} %convolution_convert_fusion), channel_id=1, source_target_pairs={{0,8},{8,0},{1,9},{9,1},{2,10},{10,2},{3,11},{11,3},{4,12},{12,4},... | collective-permute-start | bytes 7864328 | tf_op jit(solution)/shard_map/ppermute | solution.py:310
  118.8 17.1 %collective-permute-start.10 = (bf16[2,4,320,256]{3,2,1,0:T(8,128)(2,1)}, bf16[2,4,320,256]{3,2,1,0:T(8,128)(2,1)}, u32[]{:S(2)}, u32[]{:S(2)}) collective-permute-start(bf16[2,4,320,256]{3,2,1,0:T(8,128)(2,1)} %bitcast.128), channel_id=1, source_target_pairs={{0,192},{8,72},{16,208},{24,88},{32,224},{40,104},{48,240},{56,120... | collective-permute-start | bytes 3932168 | tf_op jit(solution)/shard_map/ppermute | solution.py:128
  120.3 17.8 %collective-permute-start.11 = (bf16[2,4,320,256]{3,2,1,0:T(8,128)(2,1)}, bf16[2,4,320,256]{3,2,1,0:T(8,128)(2,1)}, u32[]{:S(2)}, u32[]{:S(2)}) collective-permute-start(bf16[2,4,320,256]{3,2,1,0:T(8,128)(2,1)} %get-tuple-element.35), channel_id=1, source_target_pairs={{0,48},{8,24},{16,32},{24,8},{32,16},{40,56},{48,0},{56,40},{64,11... | collective-permute-start | bytes 3932168 | tf_op jit(solution)/shard_map/ppermute | solution.py:128
  140.1 11.7 %collective-permute-start.12 = (bf16[4,320,256]{2,1,0:T(8,128)(2,1)}, bf16[4,320,256]{2,1,0:T(8,128)(2,1)S(1)}, u32[]{:S(2)}, u32[]{:S(2)}) collective-permute-start(bf16[4,320,256]{2,1,0:T(8,128)(2,1)} %fusion.8), channel_id=1, source_target_pairs={{0,64},{8,200},{16,80},{24,216},{32,96},{40,232},{48,112},{56,248}... | collective-permute-start | bytes 1966088 | tf_op jit(solution)/shard_map/ppermute | solution.py:128
  142.5 13.3 %collective-permute-start.15 = (bf16[4,320,256]{2,1,0:T(8,128)(2,1)}, bf16[4,320,256]{2,1,0:T(8,128)(2,1)S(1)}, u32[]{:S(2)}, u32[]{:S(2)}) collective-permute-start(bf16[4,320,256]{2,1,0:T(8,128)(2,1)} %fusion.13), channel_id=1, source_target_pairs={{0,16},{8,56},{16,0},{24,40},{32,48},{40,24},{48,32},{56,8},{64,80... | collective-permute-start | bytes 1966088 | tf_op jit(solution)/shard_map/ppermute | solution.py:128
  145.1 29.7 %all-to-all-start.1 = ((bf16[32,32,512]{2,1,0:T(8,128)(2,1)}), bf16[32,32,512]{2,1,0:T(8,128)(2,1)S(1)}, u32[]{:S(2)}, u32[]{:S(2)}) async-start(bf16[32,32,512]{2,1,0:T(8,128)(2,1)} %bitcast.117), calls=%async_computation.2 | async-start | bytes 2097152 | tf_op jit(solution)/shard_map/all_to_all | solution.py:320
  154.4 14.9 %collective-permute-start.13 = (bf16[2,320,256]{2,1,0:T(8,128)(2,1)S(1)}, bf16[2,320,256]{2,1,0:T(8,128)(2,1)S(1)}, u32[]{:S(2)}, u32[]{:S(2)}) collective-permute-start(bf16[2,320,256]{2,1,0:T(8,128)(2,1)S(1)} %pad_maximum_fusion.6), channel_id=1, source_target_pairs={{0,48},{8,24},{16,32},{24,8},{32,16},{40,56},{48,0},{56,40},{64,11... | collective-permute-start | bytes 983048 | tf_op jit(solution)/shard_map/ppermute | solution.py:128
  157.3 14.6 %collective-permute-start.16 = (bf16[2,320,256]{2,1,0:T(8,128)(2,1)S(1)}, bf16[2,320,256]{2,1,0:T(8,128)(2,1)S(1)}, u32[]{:S(2)}, u32[]{:S(2)}) collective-permute-start(bf16[2,320,256]{2,1,0:T(8,128)(2,1)S(1)} %pad_maximum_fusion.7), channel_id=1, source_target_pairs={{0,192},{8,72},{16,208},{24,88},{32,224},{40,104},{48,240},{56,120... | collective-permute-start | bytes 983048 | tf_op jit(solution)/shard_map/ppermute | solution.py:128
  170.1 5.7 %collective-permute-start.14 = (bf16[320,256]{1,0:T(8,128)(2,1)}, bf16[320,256]{1,0:T(8,128)(2,1)}, u32[]{:S(2)}, u32[]{:S(2)}) collective-permute-start(bf16[320,256]{1,0:T(8,128)(2,1)} %fusion.26), channel_id=1, source_target_pairs={{0,16},{8,56},{16,0},{24,40},{32,48},{40,24},{48,32},{56,8},{64,80... | collective-permute-start | bytes 491528 | tf_op jit(solution)/shard_map/ppermute | solution.py:128
  172.7 6.7 %collective-permute-start.17 = (bf16[320,256]{1,0:T(8,128)(2,1)}, bf16[320,256]{1,0:T(8,128)(2,1)}, u32[]{:S(2)}, u32[]{:S(2)}) collective-permute-start(bf16[320,256]{1,0:T(8,128)(2,1)} %fusion.27), channel_id=1, source_target_pairs={{0,64},{8,200},{16,80},{24,216},{32,96},{40,232},{48,112},{56,248}... | collective-permute-start | bytes 491528 | tf_op jit(solution)/shard_map/ppermute | solution.py:128
  180.5 3.6 %collective-permute-start.18 = (f32[160,512]{1,0:T(8,128)S(1)}, f32[160,512]{1,0:T(8,128)}, u32[]{:S(2)}, u32[]{:S(2)}) collective-permute-start(f32[160,512]{1,0:T(8,128)S(1)} %get-tuple-element.63), channel_id=1, source_target_pairs={{0,8},{8,0},{1,9},{9,1},{2,10},{10,2},{3,11},{11,3},{4,12},{12,4},... | collective-permute-start | bytes 983048 | tf_op jit(solution)/shard_map/ppermute | solution.py:342
  (13 other events, 86.8 us)
Sparse Core Ops, SparseCore 0:
  16.3 44.2 reduce-scatter.2
  63.8 46.7 all-gather.1
  120.2 37.7 reduce-scatter.4
where the time goes:
time: 193 us
  waiting for transfers between devices  62.3 us (32%)
  starting transfers between devices  51 us (26%)
  Pallas kernels  22.8 us (12%)
  matrix products  17.2 us (9%)
  other arithmetic  16.8 us (9%)
  between operations  14.3 us (7%)
  local copies, waits for them, and re-layouts  8.29 us (4%)
    ppermute x16, waiting for transfers between devices, swap(): return lax.ppermute(array, DP, pairs)  42.8 us
    ppermute x16, starting transfers between devices, swap(): return lax.ppermute(array, DP, pairs)  27.5 us
    all_gather x1, waiting for transfers between devices, body(): merged = lax.all_gather(normed_mine, ('c', 'z'), axis=0, tiled=True)  9.07 us
    pallas_call x1, Pallas kernels, vision(): pl.pallas_call(vision_kernel, out_shape=jax.ShapeDtypeStruct((rows, width...  8.98 us
    dot_general x1, matrix products, body(): lax.dot_general(route, projected, (((0,), (0,)), ((), ())), preferred_ele...  8.51 us
    pallas_call x1, Pallas kernels, weight_blocks(): pl.pallas_call(weight_kernel, out_shape=[flat, flat, deep, deep], grid_sp...  8.26 us
    ppermute x1, starting transfers between devices, body(): given = lax.ppermute(back(pick(by_core, 1 - core)), 'c', SWAP)  6.99 us
    all_to_all x1, starting transfers between devices, body(): lax.all_to_all(outgoing.reshape(32, 32, 512), DP, split_axis=0, concat_ax...  6.69 us
  transfers between devices with their start and end apart: 24, of which 8 were waited for; matrix products, arithmetic and copies ran while one was open for 19% of the time, Pallas kernels for 3%

commit v1 on v0

--- a/solution.py
+++ b/solution.py
@@ -48,11 +48,16 @@
     layer_out = patches[...].astype(f32) + summed[...].astype(f32)
     centered = layer_out - jnp.mean(layer_out, axis=-1, keepdims=True)
     scale = lax.rsqrt(jnp.mean(centered * centered, axis=-1, keepdims=True) + epsilon)
-    normal[...] = centered * scale
+    unit = centered * scale
+    normal[...] = unit
     inverse[...] = jnp.broadcast_to(scale, inverse.shape)
-    held[...] = (normal[...] * gain[...] + shift[...]).reshape(held.shape)
+    for i in range(10):
+        at = slice(128 * i, 128 * (i + 1))
+        held[i] = unit[:, at] * gain[at] + shift[at]
     for j in range(4):
-        tokens[:, 1280 * j : 1280 * (j + 1)] = held[:, j, :].astype(bf16)
+        for i in range(10):
+            at = slice(1280 * j + 128 * i, 1280 * j + 128 * (i + 1))
+            tokens[:, at] = held[i, pl.ds(j, 32, stride=4), :].astype(bf16)
 
 
 def norm(z, patches, summed, gain, shift):
@@ -79,7 +84,7 @@
                 pl.BlockSpec((128, 1280), fixed),
                 pl.BlockSpec((128, 128), fixed),
             ],
-            scratch_shapes=[pltpu.VMEM((32, 4, 1280), f32)],
+            scratch_shapes=[pltpu.VMEM((10, 128, 128), f32)],
         ),
         compiler_params=pltpu.CompilerParams(vmem_limit_bytes=VMEM),
         name="norm",
@@ -88,8 +93,10 @@
 
 def grad_kernel(grads, normal, inverse, gain, out, held):
     for j in range(4):
-        held[:, j, :] = grads[:, 1280 * j : 1280 * (j + 1)].astype(f32)
-    scaled = held[...].reshape(128, 1280) * gain[...]
+        for i in range(10):
+            at = slice(1280 * j + 128 * i, 1280 * j + 128 * (i + 1))
+            held[i, pl.ds(j, 32, stride=4), :] = grads[:, at].astype(f32)
+    scaled = jnp.concatenate([held[i] for i in range(10)], axis=1) * gain[...]
     unit = normal[...]
     inner = jnp.mean(scaled * unit, axis=-1, keepdims=True)
     out[...] = inverse[:, :1] * (scaled - jnp.mean(scaled, axis=-1, keepdims=True) - unit * inner)
@@ -99,7 +106,7 @@
     return pl.pallas_call(
         grad_kernel,
         out_shape=jax.ShapeDtypeStruct((128, 1280), f32),
-        scratch_shapes=[pltpu.VMEM((32, 4, 1280), f32)],
+        scratch_shapes=[pltpu.VMEM((10, 128, 128), f32)],
         compiler_params=pltpu.CompilerParams(vmem_limit_bytes=VMEM),
         name="layer_grad",
     )(grads, normal, inverse, gain)
@@ -168,7 +175,7 @@
     return whole.reshape(5120, 512), after
 
 
-def weight_kernel(order, tokens, grads, give_x, keep_x, give_y, keep_y, held):
+def weight_kernel(order, tokens, grads, give_x, own_x, next_x, give_y, own_y, next_y, held):
     total = lax.dot_general(
         tokens[...], grads[...], (((0,), (0,)), ((), ())), preferred_element_type=f32
     ).astype(bf16)
@@ -177,29 +184,33 @@
     def _():
         give_x[0] = total[:, :256]
 
-    @pl.when(pl.program_id(0) >= 2)
+    @pl.when(pl.program_id(0) == 2)
     def _():
-        keep_x[0] = total[:, :256]
+        own_x[...] = total[:, :256]
+
+    @pl.when(pl.program_id(0) == 3)
+    def _():
+        next_x[...] = total[:, :256]
 
     held[...] = total[:, 256:]
 
     def rows(m):
         return held[pl.ds(pl.multiple_of(order[4 + m] * 320, 64), 320), :]
 
-    for m in range(2):
-        give_y[m, 0] = rows(m)
-        keep_y[m, 0] = rows(2 + m)
+    give_y[0, 0] = rows(0)
+    give_y[1, 0] = rows(1)
+    own_y[0] = rows(2)
+    next_y[0] = rows(3)
 
 
 def weight_blocks(tokens, grads, later):
     place, near, far = places()
     masks = jnp.stack([far, 2, 0, near])
     order = jnp.concatenate([place["x"] ^ masks, place["y"] ^ masks]).astype(jnp.int32)
-    flat = jax.ShapeDtypeStruct((2, 1280, 256), bf16)
-    deep = jax.ShapeDtypeStruct((2, 4, 320, 256), bf16)
-    give_x, keep_x, give_y, keep_y = pl.pallas_call(
+    shapes = [(2, 1280, 256)] + [(1280, 256)] * 2 + [(2, 4, 320, 256)] + [(4, 320, 256)] * 2
+    give_x, own_x, next_x, give_y, own_y, next_y = pl.pallas_call(
         weight_kernel,
-        out_shape=[flat, flat, deep, deep],
+        out_shape=[jax.ShapeDtypeStruct(shape, bf16) for shape in shapes],
         grid_spec=pltpu.PrefetchScalarGridSpec(
             num_scalar_prefetch=1,
             grid=(4,),
@@ -209,9 +220,12 @@
             ],
             out_specs=[
                 pl.BlockSpec((1, 1280, 256), lambda k, o: (jnp.minimum(k, 1), 0, 0)),
-                pl.BlockSpec((1, 1280, 256), lambda k, o: (jnp.maximum(k - 2, 0), 0, 0)),
-            ]
-            + [pl.BlockSpec((2, 1, 320, 256), lambda k, o: (0, o[k], 0, 0))] * 2,
+                pl.BlockSpec((1280, 256), lambda k, o: (0, 0)),
+                pl.BlockSpec((1280, 256), lambda k, o: (0, 0)),
+                pl.BlockSpec((2, 1, 320, 256), lambda k, o: (0, o[k], 0, 0)),
+                pl.BlockSpec((1, 320, 256), lambda k, o: (o[k], 0, 0)),
+                pl.BlockSpec((1, 320, 256), lambda k, o: (o[k], 0, 0)),
+            ],
             scratch_shapes=[pltpu.VMEM((1280, 256), bf16)],
         ),
         compiler_params=pltpu.CompilerParams(vmem_limit_bytes=VMEM),
@@ -219,22 +233,20 @@
         name="weight_product",
     )(order, tokens, grads)
     give_x, later = lax.optimization_barrier((give_x, later))
-    along_x = [p.reshape(2, 4, 320, 256) for p in (give_x, keep_x)]
-    return along_x, (give_y, keep_y), later
-
-
-def scatter_chips(blocks, later):
-    came = [swap(give, axis, 1) for (give, _), axis in zip(blocks, "xy")]
-    passed = [
-        (c[1].astype(f32) + keep[1].astype(f32)).astype(bf16) for c, (_, keep) in zip(came, blocks)
+    along_x = give_x.reshape(2, 4, 320, 256), *(p.reshape(4, 320, 256) for p in (own_x, next_x))
+    return along_x, (give_y, own_y, next_y), later
+
+
+def scatter_chips(blocks):
+    came = [swap(give, axis, 1) for (give, _, _), axis in zip(blocks, "xy")]
+    last = [
+        swap((c[1].astype(f32) + following.astype(f32)).astype(bf16), axis, 0)
+        for c, (_, _, following), axis in zip(came, blocks, "xy")
     ]
-    passed, later = lax.optimization_barrier((passed, later))
-    last = [swap(p, axis, 0) for p, axis in zip(passed, "xy")]
-    sums = [
-        (c[0].astype(f32) + keep[0].astype(f32) + end.astype(f32)).astype(bf16)
-        for c, (_, keep), end in zip(came, blocks, last)
+    return [
+        (c[0].astype(f32) + own.astype(f32) + end.astype(f32)).astype(bf16)
+        for c, (_, own, _), end in zip(came, blocks, last)
     ]
-    return sums, later
 
 
 def exchange_chips(running, earlier):
@@ -316,7 +328,7 @@
     ).astype(bf16)
 
     first_x, first_y, chip_grads = weight_blocks(merged, token_grads, chip_grads)
-    running, outgoing = scatter_chips((first_x, first_y), outgoing)
+    running = scatter_chips((first_x, first_y))
     incoming = lax.all_to_all(
         outgoing.reshape(32, 32, 512), DP, split_axis=0, concat_axis=0, tiled=True
     ).reshape(16, 2, 512 // 16, 512)

time: 193 us -> 190 us (0.984)
  other arithmetic: 16.8 us -> 13.6 us
    all_to_all x1, waiting for transfers between devices: 0.01 us -> 7.87 us  [body(): lax.all_to_all(outgoing.reshape(32, 32, 512), DP, split_axis=0, concat_ax...]
    ppermute x16, waiting for transfers between devices: 42.8 us -> 36.7 us  [swap(): return lax.ppermute(array, DP, pairs)]
  transfers between devices with their start and end apart: 24 -> 24, of which waited for: 8 -> 12; matrix products, arithmetic and copies ran while one was open for 19% -> 19% of each run, Pallas kernels for 3% -> 3%
where the time goes in v1:
time: 190 us; the launch traced here: 189 us
  waiting for transfers between devices  63.7 us (34%)
  starting transfers between devices  50.4 us (27%)
  Pallas kernels  22.2 us (12%)
  matrix products  17.5 us (9%)
  between operations  14.2 us (7%)
  other arithmetic  13.6 us (7%)
  local copies, waits for them, and re-layouts  7.26 us (4%)
    ppermute x16, waiting for transfers between devices, swap(): return lax.ppermute(array, DP, pairs)  36.7 us
    ppermute x16, starting transfers between devices, swap(): return lax.ppermute(array, DP, pairs)  25.8 us
    pallas_call x1, Pallas kernels, vision(): pl.pallas_call(vision_kernel, out_shape=jax.ShapeDtypeStruct((rows, width...  8.96 us
    all_gather x1, waiting for transfers between devices, body(): merged = lax.all_gather(normed_mine, ('c', 'z'), axis=0, tiled=True)  8.81 us
    dot_general x1, matrix products, body(): lax.dot_general(route, projected, (((0,), (0,)), ((), ())), preferred_ele...  8.51 us
    pallas_call x1, Pallas kernels, weight_blocks(): pl.pallas_call(weight_kernel, out_shape=[jax.ShapeDtypeStruct(shape, bf16...  8.5 us
    all_to_all x1, waiting for transfers between devices, body(): lax.all_to_all(outgoing.reshape(32, 32, 512), DP, split_axis=0, concat_ax...  7.87 us
    all_to_all x1, starting transfers between devices, body(): lax.all_to_all(outgoing.reshape(32, 32, 512), DP, split_axis=0, concat_ax...  7.07 us
  transfers between devices with their start and end apart: 24, of which 12 were waited for; matrix products, arithmetic and copies ran while one was open for 19% of the time, Pallas kernels for 3%

profile of v1, /device:TPU:1, one launch (start us, length us, event | category | flops | bytes accessed | tf_op | source)
XLA Modules:
  0.0 189.0 jit_solution(8381249900085213692)
XLA Ops:
  7.2 9.0 %vision.1 = bf16[1024,1280]{1,0:T(8,128)(2,1)} custom-call(bf16[1024,1280]{1,0:T(8,128)(2,1)} %patches.3, f32[1280]{0:T(1024)} %gain.3, bf16[1280,640]{1,0:T(8,128)(2,1)} %fc_in.1, bf16[640,1280]{1,0:T(8,128)(2,1)} %fc_out.1), custom_call_target="tpu_custom_call" | custom-call | flops 3355443200 | bytes 9437184 | tf_op jit(solution)/shard_map/vision/pallas_call | solution.py:34
  18.1 3.3 %collective-permute-start = (bf16[160,512]{1,0:T(8,128)(2,1)S(1)}, bf16[160,512]{1,0:T(8,128)(2,1)S(1)}, u32[]{:S(2)}, u32[]{:S(2)}) collective-permute-start(bf16[160,512]{1,0:T(8,128)(2,1)S(1)} %bitcast.130), channel_id=1, source_target_pairs={{0,8},{8,0},{1,9},{9,1},{2,10},{10,2},{3,11},{11,3},{4,12},{12,4},... | collective-permute-start | bytes 491528 | tf_op jit(solution)/shard_map/ppermute | solution.py:275
  24.2 2.6 %collective-permute-start.3 = (bf16[320,256]{1,0:T(8,128)(2,1)S(1)}, bf16[320,256]{1,0:T(8,128)(2,1)S(1)}, u32[]{:S(2)}, u32[]{:S(2)}) collective-permute-start(bf16[320,256]{1,0:T(8,128)(2,1)S(1)} %get-tuple-element.66), channel_id=1, source_target_pairs={{0,64},{8,200},{16,80},{24,216},{32,96},{40,232},{48,112},{56,248}... | collective-permute-start | bytes 491528 | tf_op jit(solution)/shard_map/ppermute | solution.py:135
  27.8 4.8 %all-to-all-start = ((bf16[32,32,512]{2,1,0:T(8,128)(2,1)}), bf16[32,32,512]{2,1,0:T(8,128)(2,1)}, u32[]{:S(2)}, u32[]{:S(2)}) async-start(bf16[32,32,512]{2,1,0:T(8,128)(2,1)} %bitcast.11), calls=%async_computation.1 | async-start | bytes 2097152 | tf_op jit(solution)/shard_map/all_to_all | solution.py:304
  35.7 14.4 %collective-permute-done.2 = bf16[2,320,256]{2,1,0:T(8,128)(2,1)S(1)} collective-permute-done((bf16[2,320,256]{2,1,0:T(8,128)(2,1)S(1)}, bf16[2,320,256]{2,1,0:T(8,128)(2,1)S(1)}, u32[]{:S(2)}, u32[]{:S(2)}) %collective-permute-start.2) | collective-permute-done | bytes 327712 | tf_op jit(solution)/shard_map/ppermute | solution.py:135
  50.2 2.5 %collective-permute-start.5 = (bf16[4,320,256]{2,1,0:T(8,128)(2,1)S(1)}, bf16[4,320,256]{2,1,0:T(8,128)(2,1)S(1)}, u32[]{:S(2)}, u32[]{:S(2)}) collective-permute-start(bf16[4,320,256]{2,1,0:T(8,128)(2,1)S(1)} %slice_dynamic-update-slice_fusion.4), channel_id=1, source_target_pairs={{0,64},{8,200},{16,80},{24,216},{32,96},{40,232},{48,112},{56,248}... | collective-permute-start | bytes 1966088 | tf_op jit(solution)/shard_map/ppermute | solution.py:135
  54.6 6.0 %reduce-scatter.3.cloned.1.call-done.summed = bf16[128,1280]{1,0:T(8,128)(2,1)} async-done(((bf16[1024,1280]{1,0:T(8,128)(2,1)}), bf16[128,1280]{1,0:T(8,128)(2,1)}) %reduce-scatter.3.cloned.1.call-update) | async-done | bytes 327696 | tf_op jit(solution)/shard_map/reduce_scatter | solution.py:279
  60.6 2.4 %norm.1 = (bf16[32,5120]{1,0:T(8,128)(2,1)}, f32[128,1280]{1,0:T(8,128)}, f32[128,128]{1,0:T(8,128)}) custom-call(s32[1]{0:T(128)} %bitcast.6.z, bf16[1024,1280]{1,0:T(8,128)(2,1)} %patches.3, bf16[128,1280]{1,0:T(8,128)(2,1)} %reduce-scatter.3.cloned.1.call-done.summed, f32[1280]{0:T(1024)} %gain.5, f32[1280]{0:T(1024)} %shift.1), custom_call_target="tpu_custom_call" | custom-call | tf_op jit(solution)/shard_map/norm/pallas_call | solution.py:66
  70.3 11.7 %collective-permute-done.7 = bf16[2,4,320,256]{3,2,1,0:T(8,128)(2,1)} collective-permute-done((bf16[2,4,320,256]{3,2,1,0:T(8,128)(2,1)}, bf16[2,4,320,256]{3,2,1,0:T(8,128)(2,1)}, u32[]{:S(2)}, u32[]{:S(2)}) %collective-permute-start.7) | collective-permute-done | bytes 1310752 | tf_op jit(solution)/shard_map/ppermute | solution.py:135
  86.3 6.5 %collective-permute-start.9 = (bf16[256,5120]{1,0:T(8,128)(2,1)S(1)}, bf16[256,5120]{1,0:T(8,128)(2,1)S(1)}, u32[]{:S(2)}, u32[]{:S(2)}) collective-permute-start(bf16[256,5120]{1,0:T(8,128)(2,1)S(1)} %convolution_convert_fusion), channel_id=1, source_target_pairs={{0,8},{8,0},{1,9},{9,1},{2,10},{10,2},{3,11},{11,3},{4,12},{12,4},... | collective-permute-start | bytes 7864328 | tf_op jit(solution)/shard_map/ppermute | solution.py:322
  93.5 4.2 %collective-permute-done.9 = bf16[256,5120]{1,0:T(8,128)(2,1)S(1)} collective-permute-done((bf16[256,5120]{1,0:T(8,128)(2,1)S(1)}, bf16[256,5120]{1,0:T(8,128)(2,1)S(1)}, u32[]{:S(2)}, u32[]{:S(2)}) %collective-permute-start.9) | collective-permute-done | bytes 2621472 | tf_op jit(solution)/shard_map/ppermute | solution.py:322
  97.7 3.3 %fusion.2 = bf16[256,5120]{1,0:T(8,128)(2,1)} fusion(bf16[5120,512]{1,0:T(8,128)(2,1)S(1)} %bitcast.111, bf16[256,5120]{1,0:T(8,128)(2,1)S(1)} %collective-permute-done.9, bf16[2,256,512]{2,1,0:T(8,128)(2,1)S(1)} %bitcast.125, s32[]{:T(128)S(6)} %select_n.128), kind=kOutput, calls=%fused_computation.4 | convolution fusion | flops 1348730880 | bytes 10747908 | tf_op jit(solution)/shard_map/dot_general | solution.py:317
  101.1 8.8 %all-gather.2.cloned.1.call-done.tokens = bf16[512,5120]{1,0:T(8,128)(2,1)} async-done(((bf16[32,5120]{1,0:T(8,128)(2,1)}), bf16[512,5120]{1,0:T(8,128)(2,1)}) %all-gather.2.cloned.1.call-update) | async-done | bytes 5242896 | tf_op jit(solution)/shard_map/all_gather | solution.py:314
  109.9 8.5 %weight_product.1 = (bf16[2,1280,256]{2,1,0:T(8,128)(2,1)}, bf16[1280,256]{1,0:T(8,128)(2,1)}, bf16[1280,256]{1,0:T(8,128)(2,1)}, bf16[2,4,320,256]{3,2,1,0:T(8,...) custom-call(s32[8]{0:T(128)} %pad_add_fusion.1.order, ...), custom_call_target="tpu_custom_call" | custom-call | flops 2684354560 | bytes 11534336 | tf_op jit(solution)/shard_map/weight_product/pallas_call | solution.py:211
  121.2 8.5 %fusion.5 = bf16[1024,512]{1,0:T(8,128)(2,1)} fusion(s32[1024]{0:T(1024)S(1)} %select_n.126, bf16[512,5120]{1,0:T(8,128)(2,1)} %all-gather.2.cloned.1.call-done.tokens, bf16[5120,512]{1,0:T(8,128)(2,1)} %bitcast.112), kind=kOutput, calls=%fused_computation.8 | convolution fusion | flops 3222536192 | bytes 11538432 | tf_op jit(solution)/shard_map/dot_general | solution.py:326
  129.7 7.1 %all-to-all-start.1 = ((bf16[32,32,512]{2,1,0:T(8,128)(2,1)}), bf16[32,32,512]{2,1,0:T(8,128)(2,1)S(1)}, u32[]{:S(2)}, u32[]{:S(2)}) async-start(bf16[32,32,512]{2,1,0:T(8,128)(2,1)} %bitcast.24), calls=%async_computation.2 | async-start | bytes 2097152 | tf_op jit(solution)/shard_map/all_to_all | solution.py:332
  136.8 2.4 %fusion.9 = bf16[4,320,256]{2,1,0:T(8,128)(2,1)} fusion(bf16[4,320,256]{2,1,0:T(8,128)(2,1)} %bitcast.122, bf16[2,4,320,256]{3,2,1,0:T(8,128)(2,1)} %collective-permute-done.10), kind=kLoop, calls=%fused_computation.17 | loop fusion | flops 1310720 | bytes 1966080 | tf_op jit(solution)/shard_map/convert_element_type | solution.py:243
  139.2 2.7 %collective-permute-start.11 = (bf16[4,320,256]{2,1,0:T(8,128)(2,1)}, bf16[4,320,256]{2,1,0:T(8,128)(2,1)}, u32[]{:S(2)}, u32[]{:S(2)}) collective-permute-start(bf16[4,320,256]{2,1,0:T(8,128)(2,1)} %fusion.9), channel_id=1, source_target_pairs={{0,64},{8,200},{16,80},{24,216},{32,96},{40,232},{48,112},{56,248}... | collective-permute-start | bytes 1966088 | tf_op jit(solution)/shard_map/ppermute | solution.py:135
  144.0 2.4 %collective-permute-start.15 = (bf16[4,320,256]{2,1,0:T(8,128)(2,1)}, bf16[4,320,256]{2,1,0:T(8,128)(2,1)}, u32[]{:S(2)}, u32[]{:S(2)}) collective-permute-start(bf16[4,320,256]{2,1,0:T(8,128)(2,1)} %fusion.6), channel_id=1, source_target_pairs={{0,16},{8,56},{16,0},{24,40},{32,48},{40,24},{48,32},{56,8},{64,80... | collective-permute-start | bytes 1966088 | tf_op jit(solution)/shard_map/ppermute | solution.py:135
  146.4 7.9 %all-to-all-done.1 = bf16[32,32,512]{2,1,0:T(8,128)(2,1)S(1)} async-done(((bf16[32,32,512]{2,1,0:T(8,128)(2,1)}), bf16[32,32,512]{2,1,0:T(8,128)(2,1)S(1)}, u32[]{:S(2)}, u32[]{:S(2)}) %all-to-all-start.1) | async-done | bytes 1048608 | tf_op jit(solution)/shard_map/all_to_all | solution.py:332
  154.3 4.8 %collective-permute-done.11 = bf16[4,320,256]{2,1,0:T(8,128)(2,1)} collective-permute-done((bf16[4,320,256]{2,1,0:T(8,128)(2,1)}, bf16[4,320,256]{2,1,0:T(8,128)(2,1)}, u32[]{:S(2)}, u32[]{:S(2)}) %collective-permute-start.11) | collective-permute-done | bytes 655392 | tf_op jit(solution)/shard_map/ppermute | solution.py:135
  164.3 3.0 %collective-permute-done.12 = bf16[2,320,256]{2,1,0:T(8,128)(2,1)S(1)} collective-permute-done((bf16[2,320,256]{2,1,0:T(8,128)(2,1)S(1)}, bf16[2,320,256]{2,1,0:T(8,128)(2,1)S(1)}, u32[]{:S(2)}, u32[]{:S(2)}) %collective-permute-start.12) | collective-permute-done | bytes 327712 | tf_op jit(solution)/shard_map/ppermute | solution.py:135
  167.4 2.5 %collective-permute-start.13 = (bf16[320,256]{1,0:T(8,128)(2,1)S(1)}, bf16[320,256]{1,0:T(8,128)(2,1)S(1)}, u32[]{:S(2)}, u32[]{:S(2)}) collective-permute-start(bf16[320,256]{1,0:T(8,128)(2,1)S(1)} %fusion.27), channel_id=1, source_target_pairs={{0,16},{8,56},{16,0},{24,40},{32,48},{40,24},{48,32},{56,8},{64,80... | collective-permute-start | bytes 491528 | tf_op jit(solution)/shard_map/ppermute | solution.py:135
  175.7 2.9 %collective-permute-start.18 = (f32[160,512]{1,0:T(8,128)S(1)}, f32[160,512]{1,0:T(8,128)}, u32[]{:S(2)}, u32[]{:S(2)}) collective-permute-start(f32[160,512]{1,0:T(8,128)S(1)} %get-tuple-element.59), channel_id=1, source_target_pairs={{0,8},{8,0},{1,9},{9,1},{2,10},{10,2},{3,11},{11,3},{4,12},{12,4},... | collective-permute-start | bytes 983048 | tf_op jit(solution)/shard_map/ppermute | solution.py:354
  (116 shorter events, 42.5 us)
Async XLA Ops:
  7.2 53.5 %reduce-scatter.3.cloned.1.call-start = ((), (), s32[]{:S(2)}) async-start(), calls=%async_computation.4 | async-start | bytes 2949120 | tf_op jit(solution)/shard_map/reduce_scatter | solution.py:279
  18.1 4.4 %collective-permute-start = (bf16[160,512]{1,0:T(8,128)(2,1)S(1)}, bf16[160,512]{1,0:T(8,128)(2,1)S(1)}, u32[]{:S(2)}, u32[]{:S(2)}) collective-permute-start(bf16[160,512]{1,0:T(8,128)(2,1)S(1)} %bitcast.130), channel_id=1, source_target_pairs={{0,8},{8,0},{1,9},{9,1},{2,10},{10,2},{3,11},{11,3},{4,12},{12,4},... | collective-permute-start | bytes 491528 | tf_op jit(solution)/shard_map/ppermute | solution.py:275
  22.6 10.1 %collective-permute-start.1 = (bf16[320,256]{1,0:T(8,128)(2,1)S(1)}, bf16[320,256]{1,0:T(8,128)(2,1)S(1)}, u32[]{:S(2)}, u32[]{:S(2)}) collective-permute-start(bf16[320,256]{1,0:T(8,128)(2,1)S(1)} %get-tuple-element.67), channel_id=1, source_target_pairs={{0,16},{8,56},{16,0},{24,40},{32,48},{40,24},{48,32},{56,8},{64,80... | collective-permute-start | bytes 491528 | tf_op jit(solution)/shard_map/ppermute | solution.py:135
  24.2 10.0 %collective-permute-start.3 = (bf16[320,256]{1,0:T(8,128)(2,1)S(1)}, bf16[320,256]{1,0:T(8,128)(2,1)S(1)}, u32[]{:S(2)}, u32[]{:S(2)}) collective-permute-start(bf16[320,256]{1,0:T(8,128)(2,1)S(1)} %get-tuple-element.66), channel_id=1, source_target_pairs={{0,64},{8,200},{16,80},{24,216},{32,96},{40,232},{48,112},{56,248}... | collective-permute-start | bytes 491528 | tf_op jit(solution)/shard_map/ppermute | solution.py:135
  27.8 26.8 %all-to-all-start = ((bf16[32,32,512]{2,1,0:T(8,128)(2,1)}), bf16[32,32,512]{2,1,0:T(8,128)(2,1)}, u32[]{:S(2)}, u32[]{:S(2)}) async-start(bf16[32,32,512]{2,1,0:T(8,128)(2,1)} %bitcast.11), calls=%async_computation.1 | async-start | bytes 2097152 | tf_op jit(solution)/shard_map/all_to_all | solution.py:304
  32.6 77.3 %all-gather.2.cloned.1.call-start = ((), (), s32[]{:S(2)}) async-start(), calls=%async_computation.5 | async-start | bytes 5570560 | tf_op jit(solution)/shard_map/all_gather | solution.py:314
  32.7 17.4 %collective-permute-start.2 = (bf16[2,320,256]{2,1,0:T(8,128)(2,1)S(1)}, bf16[2,320,256]{2,1,0:T(8,128)(2,1)S(1)}, u32[]{:S(2)}, u32[]{:S(2)}) collective-permute-start(bf16[2,320,256]{2,1,0:T(8,128)(2,1)S(1)} %pad_maximum_fusion.4), channel_id=1, source_target_pairs={{0,48},{8,24},{16,32},{24,8},{32,16},{40,56},{48,0},{56,40},{64,11... | collective-permute-start | bytes 983048 | tf_op jit(solution)/shard_map/ppermute | solution.py:135
  34.3 18.4 %collective-permute-start.4 = (bf16[2,320,256]{2,1,0:T(8,128)(2,1)S(1)}, bf16[2,320,256]{2,1,0:T(8,128)(2,1)S(1)}, u32[]{:S(2)}, u32[]{:S(2)}) collective-permute-start(bf16[2,320,256]{2,1,0:T(8,128)(2,1)S(1)} %pad_maximum_fusion.5), channel_id=1, source_target_pairs={{0,192},{8,72},{16,208},{24,88},{32,224},{40,104},{48,240},{56,120... | collective-permute-start | bytes 983048 | tf_op jit(solution)/shard_map/ppermute | solution.py:135
  50.2 12.9 %collective-permute-start.5 = (bf16[4,320,256]{2,1,0:T(8,128)(2,1)S(1)}, bf16[4,320,256]{2,1,0:T(8,128)(2,1)S(1)}, u32[]{:S(2)}, u32[]{:S(2)}) collective-permute-start(bf16[4,320,256]{2,1,0:T(8,128)(2,1)S(1)} %slice_dynamic-update-slice_fusion.4), channel_id=1, source_target_pairs={{0,64},{8,200},{16,80},{24,216},{32,96},{40,232},{48,112},{56,248}... | collective-permute-start | bytes 1966088 | tf_op jit(solution)/shard_map/ppermute | solution.py:135
  52.7 10.7 %collective-permute-start.6 = (bf16[4,320,256]{2,1,0:T(8,128)(2,1)S(1)}, bf16[4,320,256]{2,1,0:T(8,128)(2,1)S(1)}, u32[]{:S(2)}, u32[]{:S(2)}) collective-permute-start(bf16[4,320,256]{2,1,0:T(8,128)(2,1)S(1)} %slice_dynamic-update-slice_fusion.2), channel_id=1, source_target_pairs={{0,16},{8,56},{16,0},{24,40},{32,48},{40,24},{48,32},{56,8},{64,80... | collective-permute-start | bytes 1966088 | tf_op jit(solution)/shard_map/ppermute | solution.py:135
  63.5 109.5 %reduce-scatter.5.cloned.1.call-start = ((), (), s32[]{:S(2)}) async-start(), calls=%async_computation.6 | async-start | bytes 2949120 | tf_op jit(solution)/shard_map/reduce_scatter | solution.py:348
  65.0 17.1 %collective-permute-start.7 = (bf16[2,4,320,256]{3,2,1,0:T(8,128)(2,1)}, bf16[2,4,320,256]{3,2,1,0:T(8,128)(2,1)}, u32[]{:S(2)}, u32[]{:S(2)}) collective-permute-start(bf16[2,4,320,256]{3,2,1,0:T(8,128)(2,1)} %pad_maximum_fusion), channel_id=1, source_target_pairs={{0,192},{8,72},{16,208},{24,88},{32,224},{40,104},{48,240},{56,120... | collective-permute-start | bytes 3932168 | tf_op jit(solution)/shard_map/ppermute | solution.py:135
  66.3 18.2 %collective-permute-start.8 = (bf16[2,4,320,256]{3,2,1,0:T(8,128)(2,1)S(1)}, bf16[2,4,320,256]{3,2,1,0:T(8,128)(2,1)S(1)}, u32[]{:S(2)}, u32[]{:S(2)}) collective-permute-start(bf16[2,4,320,256]{3,2,1,0:T(8,128)(2,1)S(1)} %pad_maximum_fusion.1), channel_id=1, source_target_pairs={{0,48},{8,24},{16,32},{24,8},{32,16},{40,56},{48,0},{56,40},{64,11... | collective-permute-start | bytes 3932168 | tf_op jit(solution)/shard_map/ppermute | solution.py:135
  86.3 11.4 %collective-permute-start.9 = (bf16[256,5120]{1,0:T(8,128)(2,1)S(1)}, bf16[256,5120]{1,0:T(8,128)(2,1)S(1)}, u32[]{:S(2)}, u32[]{:S(2)}) collective-permute-start(bf16[256,5120]{1,0:T(8,128)(2,1)S(1)} %convolution_convert_fusion), channel_id=1, source_target_pairs={{0,8},{8,0},{1,9},{9,1},{2,10},{10,2},{3,11},{11,3},{4,12},{12,4},... | collective-permute-start | bytes 7864328 | tf_op jit(solution)/shard_map/ppermute | solution.py:322
  118.4 23.5 %collective-permute-start.14 = (bf16[2,4,320,256]{3,2,1,0:T(8,128)(2,1)}, bf16[2,4,320,256]{3,2,1,0:T(8,128)(2,1)S(1)}, u32[]{:S(2)}, u32[]{:S(2)}) collective-permute-start(bf16[2,4,320,256]{3,2,1,0:T(8,128)(2,1)} %get-tuple-element.35), channel_id=1, source_target_pairs={{0,48},{8,24},{16,32},{24,8},{32,16},{40,56},{48,0},{56,40},{64,11... | collective-permute-start | bytes 3932168 | tf_op jit(solution)/shard_map/ppermute | solution.py:135
  119.8 17.1 %collective-permute-start.10 = (bf16[2,4,320,256]{3,2,1,0:T(8,128)(2,1)}, bf16[2,4,320,256]{3,2,1,0:T(8,128)(2,1)}, u32[]{:S(2)}, u32[]{:S(2)}) collective-permute-start(bf16[2,4,320,256]{3,2,1,0:T(8,128)(2,1)} %bitcast.34), channel_id=1, source_target_pairs={{0,192},{8,72},{16,208},{24,88},{32,224},{40,104},{48,240},{56,120... | collective-permute-start | bytes 3932168 | tf_op jit(solution)/shard_map/ppermute | solution.py:135
  129.7 24.6 %all-to-all-start.1 = ((bf16[32,32,512]{2,1,0:T(8,128)(2,1)}), bf16[32,32,512]{2,1,0:T(8,128)(2,1)S(1)}, u32[]{:S(2)}, u32[]{:S(2)}) async-start(bf16[32,32,512]{2,1,0:T(8,128)(2,1)} %bitcast.24), calls=%async_computation.2 | async-start | bytes 2097152 | tf_op jit(solution)/shard_map/all_to_all | solution.py:332
  139.2 20.0 %collective-permute-start.11 = (bf16[4,320,256]{2,1,0:T(8,128)(2,1)}, bf16[4,320,256]{2,1,0:T(8,128)(2,1)}, u32[]{:S(2)}, u32[]{:S(2)}) collective-permute-start(bf16[4,320,256]{2,1,0:T(8,128)(2,1)} %fusion.9), channel_id=1, source_target_pairs={{0,64},{8,200},{16,80},{24,216},{32,96},{40,232},{48,112},{56,248}... | collective-permute-start | bytes 1966088 | tf_op jit(solution)/shard_map/ppermute | solution.py:135
  144.0 18.1 %collective-permute-start.15 = (bf16[4,320,256]{2,1,0:T(8,128)(2,1)}, bf16[4,320,256]{2,1,0:T(8,128)(2,1)}, u32[]{:S(2)}, u32[]{:S(2)}) collective-permute-start(bf16[4,320,256]{2,1,0:T(8,128)(2,1)} %fusion.6), channel_id=1, source_target_pairs={{0,16},{8,56},{16,0},{24,40},{32,48},{40,24},{48,32},{56,8},{64,80... | collective-permute-start | bytes 1966088 | tf_op jit(solution)/shard_map/ppermute | solution.py:135
  160.8 6.5 %collective-permute-start.12 = (bf16[2,320,256]{2,1,0:T(8,128)(2,1)S(1)}, bf16[2,320,256]{2,1,0:T(8,128)(2,1)S(1)}, u32[]{:S(2)}, u32[]{:S(2)}) collective-permute-start(bf16[2,320,256]{2,1,0:T(8,128)(2,1)S(1)} %pad_maximum_fusion.6), channel_id=1, source_target_pairs={{0,48},{8,24},{16,32},{24,8},{32,16},{40,56},{48,0},{56,40},{64,11... | collective-permute-start | bytes 983048 | tf_op jit(solution)/shard_map/ppermute | solution.py:135
  163.5 6.5 %collective-permute-start.16 = (bf16[2,320,256]{2,1,0:T(8,128)(2,1)S(1)}, bf16[2,320,256]{2,1,0:T(8,128)(2,1)S(1)}, u32[]{:S(2)}, u32[]{:S(2)}) collective-permute-start(bf16[2,320,256]{2,1,0:T(8,128)(2,1)S(1)} %pad_maximum_fusion.7), channel_id=1, source_target_pairs={{0,192},{8,72},{16,208},{24,88},{32,224},{40,104},{48,240},{56,120... | collective-permute-start | bytes 983048 | tf_op jit(solution)/shard_map/ppermute | solution.py:135
  167.4 5.5 %collective-permute-start.13 = (bf16[320,256]{1,0:T(8,128)(2,1)S(1)}, bf16[320,256]{1,0:T(8,128)(2,1)S(1)}, u32[]{:S(2)}, u32[]{:S(2)}) collective-permute-start(bf16[320,256]{1,0:T(8,128)(2,1)S(1)} %fusion.27), channel_id=1, source_target_pairs={{0,16},{8,56},{16,0},{24,40},{32,48},{40,24},{48,32},{56,8},{64,80... | collective-permute-start | bytes 491528 | tf_op jit(solution)/shard_map/ppermute | solution.py:135
  170.0 5.5 %collective-permute-start.17 = (bf16[320,256]{1,0:T(8,128)(2,1)S(1)}, bf16[320,256]{1,0:T(8,128)(2,1)S(1)}, u32[]{:S(2)}, u32[]{:S(2)}) collective-permute-start(bf16[320,256]{1,0:T(8,128)(2,1)S(1)} %fusion.28), channel_id=1, source_target_pairs={{0,64},{8,200},{16,80},{24,216},{32,96},{40,232},{48,112},{56,248}... | collective-permute-start | bytes 491528 | tf_op jit(solution)/shard_map/ppermute | solution.py:135
  175.7 4.8 %collective-permute-start.18 = (f32[160,512]{1,0:T(8,128)S(1)}, f32[160,512]{1,0:T(8,128)}, u32[]{:S(2)}, u32[]{:S(2)}) collective-permute-start(f32[160,512]{1,0:T(8,128)S(1)} %get-tuple-element.59), channel_id=1, source_target_pairs={{0,8},{8,0},{1,9},{9,1},{2,10},{10,2},{3,11},{11,3},{4,12},{12,4},... | collective-permute-start | bytes 983048 | tf_op jit(solution)/shard_map/ppermute | solution.py:354
  (7 other events, 82.7 us)
Sparse Core Ops, SparseCore 0:
  16.3 44.2 reduce-scatter.2
  63.6 46.2 all-gather.1
  118.5 38.4 reduce-scatter.4

commit v2 on v1

--- a/solution.py
+++ b/solution.py
@@ -349,15 +349,15 @@
     grad_layer = layer_grad(merged_grads, normal, inverse, merge_gain)
 
     sums, grad_layer = exchange_chips(running, grad_layer)
-    chip_rows = jnp.concatenate(sums, axis=1).reshape(2, 160, 512) * (1.0 / math.sqrt(8192))
-    mine = pick(chip_rows, core)
-    other = lax.ppermute(
-        pick(chip_rows, 1 - core), "c", SWAP
-    )
+    mine, other = [], []
+    for part in sums:
+        rows = part.reshape(2, 160, 256) * (1.0 / math.sqrt(8192))
+        mine.append(pick(rows, core))
+        other.append(lax.ppermute(pick(rows, 1 - core), "c", SWAP))
     grad_weight = jnp.where(
         core == 0,
-        jnp.concatenate([mine, other], axis=1),
-        jnp.concatenate([other, mine], axis=1),
+        jnp.concatenate(mine + other, axis=1),
+        jnp.concatenate(other + mine, axis=1),
     )
     return (visual, grad_weight, grad_layer)
 

time: 190 us -> 190 us (level)
  transfers between devices with their start and end apart: 24 -> 25, of which waited for: 12 -> 12; matrix products, arithmetic and copies ran while one was open for 19% -> 19% of each run, Pallas kernels for 3% -> 3%
where the time goes in v2:
time: 190 us; the launch traced here: 189 us
  waiting for transfers between devices  63.9 us (34%)
  starting transfers between devices  49.5 us (26%)
  Pallas kernels  22.2 us (12%)
  matrix products  17.5 us (9%)
  between operations  14.2 us (7%)
  other arithmetic  13.5 us (7%)
  local copies, waits for them, and re-layouts  7.93 us (4%)
    ppermute x16, waiting for transfers between devices, swap(): return lax.ppermute(array, DP, pairs)  37 us
    ppermute x16, starting transfers between devices, swap(): return lax.ppermute(array, DP, pairs)  25.4 us
    pallas_call x1, Pallas kernels, vision(): pl.pallas_call(vision_kernel, out_shape=jax.ShapeDtypeStruct((rows, width...  8.97 us
    all_gather x1, waiting for transfers between devices, body(): merged = lax.all_gather(normed_mine, ('c', 'z'), axis=0, tiled=True)  8.85 us
    dot_general x1, matrix products, body(): lax.dot_general(route, projected, (((0,), (0,)), ((), ())), preferred_ele...  8.51 us
    pallas_call x1, Pallas kernels, weight_blocks(): pl.pallas_call(weight_kernel, out_shape=[jax.ShapeDtypeStruct(shape, bf16...  8.47 us
    all_to_all x1, waiting for transfers between devices, body(): lax.all_to_all(outgoing.reshape(32, 32, 512), DP, split_axis=0, concat_ax...  7.86 us
    all_to_all x1, starting transfers between devices, body(): lax.all_to_all(outgoing.reshape(32, 32, 512), DP, split_axis=0, concat_ax...  7.05 us
  transfers between devices with their start and end apart: 25, of which 12 were waited for; matrix products, arithmetic and copies ran while one was open for 19% of the time, Pallas kernels for 3%

profile of v2, /device:TPU:1, one launch (start us, length us, event | category | flops | bytes accessed | tf_op | source)
XLA Modules:
  0.0 188.8 jit_solution(12115862159508444878)
XLA Ops:
  7.2 9.0 %vision.1 = bf16[1024,1280]{1,0:T(8,128)(2,1)} custom-call(bf16[1024,1280]{1,0:T(8,128)(2,1)} %patches.3, f32[1280]{0:T(1024)} %gain.3, bf16[1280,640]{1,0:T(8,128)(2,1)} %fc_in.1, bf16[640,1280]{1,0:T(8,128)(2,1)} %fc_out.1), custom_call_target="tpu_custom_call" | custom-call | flops 3355443200 | bytes 9437184 | tf_op jit(solution)/shard_map/vision/pallas_call | solution.py:34
  18.1 3.3 %collective-permute-start = (bf16[160,512]{1,0:T(8,128)(2,1)S(1)}, bf16[160,512]{1,0:T(8,128)(2,1)S(1)}, u32[]{:S(2)}, u32[]{:S(2)}) collective-permute-start(bf16[160,512]{1,0:T(8,128)(2,1)S(1)} %bitcast.140), channel_id=1, source_target_pairs={{0,8},{8,0},{1,9},{9,1},{2,10},{10,2},{3,11},{11,3},{4,12},{12,4},... | collective-permute-start | bytes 491528 | tf_op jit(solution)/shard_map/ppermute | solution.py:275
  24.2 2.6 %collective-permute-start.3 = (bf16[320,256]{1,0:T(8,128)(2,1)S(1)}, bf16[320,256]{1,0:T(8,128)(2,1)S(1)}, u32[]{:S(2)}, u32[]{:S(2)}) collective-permute-start(bf16[320,256]{1,0:T(8,128)(2,1)S(1)} %get-tuple-element.68), channel_id=1, source_target_pairs={{0,64},{8,200},{16,80},{24,216},{32,96},{40,232},{48,112},{56,248}... | collective-permute-start | bytes 491528 | tf_op jit(solution)/shard_map/ppermute | solution.py:135
  27.8 4.8 %all-to-all-start = ((bf16[32,32,512]{2,1,0:T(8,128)(2,1)}), bf16[32,32,512]{2,1,0:T(8,128)(2,1)}, u32[]{:S(2)}, u32[]{:S(2)}) async-start(bf16[32,32,512]{2,1,0:T(8,128)(2,1)} %bitcast.11), calls=%async_computation.1 | async-start | bytes 2097152 | tf_op jit(solution)/shard_map/all_to_all | solution.py:304
  35.7 14.4 %collective-permute-done.2 = bf16[2,320,256]{2,1,0:T(8,128)(2,1)S(1)} collective-permute-done((bf16[2,320,256]{2,1,0:T(8,128)(2,1)S(1)}, bf16[2,320,256]{2,1,0:T(8,128)(2,1)S(1)}, u32[]{:S(2)}, u32[]{:S(2)}) %collective-permute-start.2) | collective-permute-done | bytes 327712 | tf_op jit(solution)/shard_map/ppermute | solution.py:135
  50.2 2.5 %collective-permute-start.5 = (bf16[4,320,256]{2,1,0:T(8,128)(2,1)S(1)}, bf16[4,320,256]{2,1,0:T(8,128)(2,1)S(1)}, u32[]{:S(2)}, u32[]{:S(2)}) collective-permute-start(bf16[4,320,256]{2,1,0:T(8,128)(2,1)S(1)} %slice_dynamic-update-slice_fusion.4), channel_id=1, source_target_pairs={{0,64},{8,200},{16,80},{24,216},{32,96},{40,232},{48,112},{56,248}... | collective-permute-start | bytes 1966088 | tf_op jit(solution)/shard_map/ppermute | solution.py:135
  54.6 6.0 %reduce-scatter.3.cloned.1.call-done.summed = bf16[128,1280]{1,0:T(8,128)(2,1)} async-done(((bf16[1024,1280]{1,0:T(8,128)(2,1)}), bf16[128,1280]{1,0:T(8,128)(2,1)}) %reduce-scatter.3.cloned.1.call-update) | async-done | bytes 327696 | tf_op jit(solution)/shard_map/reduce_scatter | solution.py:279
  60.7 2.4 %norm.1 = (bf16[32,5120]{1,0:T(8,128)(2,1)}, f32[128,1280]{1,0:T(8,128)}, f32[128,128]{1,0:T(8,128)}) custom-call(s32[1]{0:T(128)} %bitcast.6.z, bf16[1024,1280]{1,0:T(8,128)(2,1)} %patches.3, bf16[128,1280]{1,0:T(8,128)(2,1)} %reduce-scatter.3.cloned.1.call-done.summed, f32[1280]{0:T(1024)} %gain.5, f32[1280]{0:T(1024)} %shift.1), custom_call_target="tpu_custom_call" | custom-call | tf_op jit(solution)/shard_map/norm/pallas_call | solution.py:66
  70.3 11.7 %collective-permute-done.7 = bf16[2,4,320,256]{3,2,1,0:T(8,128)(2,1)} collective-permute-done((bf16[2,4,320,256]{3,2,1,0:T(8,128)(2,1)}, bf16[2,4,320,256]{3,2,1,0:T(8,128)(2,1)}, u32[]{:S(2)}, u32[]{:S(2)}) %collective-permute-start.7) | collective-permute-done | bytes 1310752 | tf_op jit(solution)/shard_map/ppermute | solution.py:135
  86.3 6.5 %collective-permute-start.9 = (bf16[256,5120]{1,0:T(8,128)(2,1)S(1)}, bf16[256,5120]{1,0:T(8,128)(2,1)S(1)}, u32[]{:S(2)}, u32[]{:S(2)}) collective-permute-start(bf16[256,5120]{1,0:T(8,128)(2,1)S(1)} %convolution_convert_fusion), channel_id=1, source_target_pairs={{0,8},{8,0},{1,9},{9,1},{2,10},{10,2},{3,11},{11,3},{4,12},{12,4},... | collective-permute-start | bytes 7864328 | tf_op jit(solution)/shard_map/ppermute | solution.py:322
  93.5 4.2 %collective-permute-done.9 = bf16[256,5120]{1,0:T(8,128)(2,1)S(1)} collective-permute-done((bf16[256,5120]{1,0:T(8,128)(2,1)S(1)}, bf16[256,5120]{1,0:T(8,128)(2,1)S(1)}, u32[]{:S(2)}, u32[]{:S(2)}) %collective-permute-start.9) | collective-permute-done | bytes 2621472 | tf_op jit(solution)/shard_map/ppermute | solution.py:322
  97.7 3.3 %fusion.2 = bf16[256,5120]{1,0:T(8,128)(2,1)} fusion(bf16[5120,512]{1,0:T(8,128)(2,1)S(1)} %bitcast.120, bf16[256,5120]{1,0:T(8,128)(2,1)S(1)} %collective-permute-done.9, bf16[2,256,512]{2,1,0:T(8,128)(2,1)S(1)} %bitcast.135, s32[]{:T(128)S(6)} %select_n.130), kind=kOutput, calls=%fused_computation.4 | convolution fusion | flops 1348730880 | bytes 10747908 | tf_op jit(solution)/shard_map/dot_general | solution.py:317
  101.0 8.8 %all-gather.2.cloned.1.call-done.tokens = bf16[512,5120]{1,0:T(8,128)(2,1)} async-done(((bf16[32,5120]{1,0:T(8,128)(2,1)}), bf16[512,5120]{1,0:T(8,128)(2,1)}) %all-gather.2.cloned.1.call-update) | async-done | bytes 5242896 | tf_op jit(solution)/shard_map/all_gather | solution.py:314
  109.9 8.5 %weight_product.1 = (bf16[2,1280,256]{2,1,0:T(8,128)(2,1)}, bf16[1280,256]{1,0:T(8,128)(2,1)}, bf16[1280,256]{1,0:T(8,128)(2,1)}, bf16[2,4,320,256]{3,2,1,0:T(8,...) custom-call(s32[8]{0:T(128)} %pad_add_fusion.1.order, ...), custom_call_target="tpu_custom_call" | custom-call | flops 2684354560 | bytes 11534336 | tf_op jit(solution)/shard_map/weight_product/pallas_call | solution.py:211
  121.2 8.5 %fusion.5 = bf16[1024,512]{1,0:T(8,128)(2,1)} fusion(s32[1024]{0:T(1024)S(1)} %select_n.128, bf16[512,5120]{1,0:T(8,128)(2,1)} %all-gather.2.cloned.1.call-done.tokens, bf16[5120,512]{1,0:T(8,128)(2,1)} %bitcast.121), kind=kOutput, calls=%fused_computation.8 | convolution fusion | flops 3222536192 | bytes 11538432 | tf_op jit(solution)/shard_map/dot_general | solution.py:326
  129.7 7.0 %all-to-all-start.1 = ((bf16[32,32,512]{2,1,0:T(8,128)(2,1)}), bf16[32,32,512]{2,1,0:T(8,128)(2,1)S(1)}, u32[]{:S(2)}, u32[]{:S(2)}) async-start(bf16[32,32,512]{2,1,0:T(8,128)(2,1)} %bitcast.24), calls=%async_computation.2 | async-start | bytes 2097152 | tf_op jit(solution)/shard_map/all_to_all | solution.py:332
  136.9 2.4 %fusion.9 = bf16[4,320,256]{2,1,0:T(8,128)(2,1)} fusion(bf16[4,320,256]{2,1,0:T(8,128)(2,1)} %bitcast.132, bf16[2,4,320,256]{3,2,1,0:T(8,128)(2,1)} %collective-permute-done.10), kind=kLoop, calls=%fused_computation.17 | loop fusion | flops 1310720 | bytes 1966080 | tf_op jit(solution)/shard_map/convert_element_type | solution.py:243
  139.3 2.6 %collective-permute-start.11 = (bf16[4,320,256]{2,1,0:T(8,128)(2,1)}, bf16[4,320,256]{2,1,0:T(8,128)(2,1)}, u32[]{:S(2)}, u32[]{:S(2)}) collective-permute-start(bf16[4,320,256]{2,1,0:T(8,128)(2,1)} %fusion.9), channel_id=1, source_target_pairs={{0,64},{8,200},{16,80},{24,216},{32,96},{40,232},{48,112},{56,248}... | collective-permute-start | bytes 1966088 | tf_op jit(solution)/shard_map/ppermute | solution.py:135
  144.0 2.4 %collective-permute-start.15 = (bf16[4,320,256]{2,1,0:T(8,128)(2,1)}, bf16[4,320,256]{2,1,0:T(8,128)(2,1)}, u32[]{:S(2)}, u32[]{:S(2)}) collective-permute-start(bf16[4,320,256]{2,1,0:T(8,128)(2,1)} %fusion.6), channel_id=1, source_target_pairs={{0,16},{8,56},{16,0},{24,40},{32,48},{40,24},{48,32},{56,8},{64,80... | collective-permute-start | bytes 1966088 | tf_op jit(solution)/shard_map/ppermute | solution.py:135
  146.4 7.9 %all-to-all-done.1 = bf16[32,32,512]{2,1,0:T(8,128)(2,1)S(1)} async-done(((bf16[32,32,512]{2,1,0:T(8,128)(2,1)}), bf16[32,32,512]{2,1,0:T(8,128)(2,1)S(1)}, u32[]{:S(2)}, u32[]{:S(2)}) %all-to-all-start.1) | async-done | bytes 1048608 | tf_op jit(solution)/shard_map/all_to_all | solution.py:332
  154.3 4.8 %collective-permute-done.11 = bf16[4,320,256]{2,1,0:T(8,128)(2,1)} collective-permute-done((bf16[4,320,256]{2,1,0:T(8,128)(2,1)}, bf16[4,320,256]{2,1,0:T(8,128)(2,1)}, u32[]{:S(2)}, u32[]{:S(2)}) %collective-permute-start.11) | collective-permute-done | bytes 655392 | tf_op jit(solution)/shard_map/ppermute | solution.py:135
  164.4 2.9 %collective-permute-done.12 = bf16[2,320,256]{2,1,0:T(8,128)(2,1)S(1)} collective-permute-done((bf16[2,320,256]{2,1,0:T(8,128)(2,1)S(1)}, bf16[2,320,256]{2,1,0:T(8,128)(2,1)S(1)}, u32[]{:S(2)}, u32[]{:S(2)}) %collective-permute-start.12) | collective-permute-done | bytes 327712 | tf_op jit(solution)/shard_map/ppermute | solution.py:135
  167.4 2.2 %collective-permute-start.13 = (bf16[320,256]{1,0:T(8,128)(2,1)S(1)}, bf16[320,256]{1,0:T(8,128)(2,1)S(1)}, u32[]{:S(2)}, u32[]{:S(2)}) collective-permute-start(bf16[320,256]{1,0:T(8,128)(2,1)S(1)} %fusion.29), channel_id=1, source_target_pairs={{0,16},{8,56},{16,0},{24,40},{32,48},{40,24},{48,32},{56,8},{64,80... | collective-permute-start | bytes 491528 | tf_op jit(solution)/shard_map/ppermute | solution.py:135
  174.7 2.4 %layer_grad.1 = f32[128,1280]{1,0:T(8,128)} custom-call(bf16[32,5120]{1,0:T(8,128)(2,1)} %reduce-scatter.5.cloned.1.call-done.grads, f32[128,1280]{1,0:T(8,128)} %get-tuple-element.39.normal, f32[128,128]{1,0:T(8,128)} %get-tuple-element.40.inverse, f32[1280]{0:T(1024)} %gain.5), custom_call_target="tpu_custom_call" | custom-call | tf_op jit(solution)/shard_map/layer_grad/pallas_call | solution.py:106
  (118 shorter events, 43.3 us)
Async XLA Ops:
  7.2 53.5 %reduce-scatter.3.cloned.1.call-start = ((), (), s32[]{:S(2)}) async-start(), calls=%async_computation.4 | async-start | bytes 2949120 | tf_op jit(solution)/shard_map/reduce_scatter | solution.py:279
  18.1 4.4 %collective-permute-start = (bf16[160,512]{1,0:T(8,128)(2,1)S(1)}, bf16[160,512]{1,0:T(8,128)(2,1)S(1)}, u32[]{:S(2)}, u32[]{:S(2)}) collective-permute-start(bf16[160,512]{1,0:T(8,128)(2,1)S(1)} %bitcast.140), channel_id=1, source_target_pairs={{0,8},{8,0},{1,9},{9,1},{2,10},{10,2},{3,11},{11,3},{4,12},{12,4},... | collective-permute-start | bytes 491528 | tf_op jit(solution)/shard_map/ppermute | solution.py:275
  22.6 10.1 %collective-permute-start.1 = (bf16[320,256]{1,0:T(8,128)(2,1)S(1)}, bf16[320,256]{1,0:T(8,128)(2,1)S(1)}, u32[]{:S(2)}, u32[]{:S(2)}) collective-permute-start(bf16[320,256]{1,0:T(8,128)(2,1)S(1)} %get-tuple-element.69), channel_id=1, source_target_pairs={{0,16},{8,56},{16,0},{24,40},{32,48},{40,24},{48,32},{56,8},{64,80... | collective-permute-start | bytes 491528 | tf_op jit(solution)/shard_map/ppermute | solution.py:135
  24.2 10.0 %collective-permute-start.3 = (bf16[320,256]{1,0:T(8,128)(2,1)S(1)}, bf16[320,256]{1,0:T(8,128)(2,1)S(1)}, u32[]{:S(2)}, u32[]{:S(2)}) collective-permute-start(bf16[320,256]{1,0:T(8,128)(2,1)S(1)} %get-tuple-element.68), channel_id=1, source_target_pairs={{0,64},{8,200},{16,80},{24,216},{32,96},{40,232},{48,112},{56,248}... | collective-permute-start | bytes 491528 | tf_op jit(solution)/shard_map/ppermute | solution.py:135
  27.8 26.8 %all-to-all-start = ((bf16[32,32,512]{2,1,0:T(8,128)(2,1)}), bf16[32,32,512]{2,1,0:T(8,128)(2,1)}, u32[]{:S(2)}, u32[]{:S(2)}) async-start(bf16[32,32,512]{2,1,0:T(8,128)(2,1)} %bitcast.11), calls=%async_computation.1 | async-start | bytes 2097152 | tf_op jit(solution)/shard_map/all_to_all | solution.py:304
  32.6 77.3 %all-gather.2.cloned.1.call-start = ((), (), s32[]{:S(2)}) async-start(), calls=%async_computation.5 | async-start | bytes 5570560 | tf_op jit(solution)/shard_map/all_gather | solution.py:314
  32.8 17.4 %collective-permute-start.2 = (bf16[2,320,256]{2,1,0:T(8,128)(2,1)S(1)}, bf16[2,320,256]{2,1,0:T(8,128)(2,1)S(1)}, u32[]{:S(2)}, u32[]{:S(2)}) collective-permute-start(bf16[2,320,256]{2,1,0:T(8,128)(2,1)S(1)} %pad_maximum_fusion.4), channel_id=1, source_target_pairs={{0,48},{8,24},{16,32},{24,8},{32,16},{40,56},{48,0},{56,40},{64,11... | collective-permute-start | bytes 983048 | tf_op jit(solution)/shard_map/ppermute | solution.py:135
  34.3 18.4 %collective-permute-start.4 = (bf16[2,320,256]{2,1,0:T(8,128)(2,1)S(1)}, bf16[2,320,256]{2,1,0:T(8,128)(2,1)S(1)}, u32[]{:S(2)}, u32[]{:S(2)}) collective-permute-start(bf16[2,320,256]{2,1,0:T(8,128)(2,1)S(1)} %pad_maximum_fusion.5), channel_id=1, source_target_pairs={{0,192},{8,72},{16,208},{24,88},{32,224},{40,104},{48,240},{56,120... | collective-permute-start | bytes 983048 | tf_op jit(solution)/shard_map/ppermute | solution.py:135
  50.2 12.9 %collective-permute-start.5 = (bf16[4,320,256]{2,1,0:T(8,128)(2,1)S(1)}, bf16[4,320,256]{2,1,0:T(8,128)(2,1)S(1)}, u32[]{:S(2)}, u32[]{:S(2)}) collective-permute-start(bf16[4,320,256]{2,1,0:T(8,128)(2,1)S(1)} %slice_dynamic-update-slice_fusion.4), channel_id=1, source_target_pairs={{0,64},{8,200},{16,80},{24,216},{32,96},{40,232},{48,112},{56,248}... | collective-permute-start | bytes 1966088 | tf_op jit(solution)/shard_map/ppermute | solution.py:135
  52.8 10.7 %collective-permute-start.6 = (bf16[4,320,256]{2,1,0:T(8,128)(2,1)S(1)}, bf16[4,320,256]{2,1,0:T(8,128)(2,1)S(1)}, u32[]{:S(2)}, u32[]{:S(2)}) collective-permute-start(bf16[4,320,256]{2,1,0:T(8,128)(2,1)S(1)} %slice_dynamic-update-slice_fusion.2), channel_id=1, source_target_pairs={{0,16},{8,56},{16,0},{24,40},{32,48},{40,24},{48,32},{56,8},{64,80... | collective-permute-start | bytes 1966088 | tf_op jit(solution)/shard_map/ppermute | solution.py:135
  63.5 111.2 %reduce-scatter.5.cloned.1.call-start = ((), (), s32[]{:S(2)}) async-start(), calls=%async_computation.6 | async-start | bytes 2949120 | tf_op jit(solution)/shard_map/reduce_scatter | solution.py:348
  65.0 17.1 %collective-permute-start.7 = (bf16[2,4,320,256]{3,2,1,0:T(8,128)(2,1)}, bf16[2,4,320,256]{3,2,1,0:T(8,128)(2,1)}, u32[]{:S(2)}, u32[]{:S(2)}) collective-permute-start(bf16[2,4,320,256]{3,2,1,0:T(8,128)(2,1)} %pad_maximum_fusion), channel_id=1, source_target_pairs={{0,192},{8,72},{16,208},{24,88},{32,224},{40,104},{48,240},{56,120... | collective-permute-start | bytes 3932168 | tf_op jit(solution)/shard_map/ppermute | solution.py:135
  66.3 18.2 %collective-permute-start.8 = (bf16[2,4,320,256]{3,2,1,0:T(8,128)(2,1)S(1)}, bf16[2,4,320,256]{3,2,1,0:T(8,128)(2,1)S(1)}, u32[]{:S(2)}, u32[]{:S(2)}) collective-permute-start(bf16[2,4,320,256]{3,2,1,0:T(8,128)(2,1)S(1)} %pad_maximum_fusion.1), channel_id=1, source_target_pairs={{0,48},{8,24},{16,32},{24,8},{32,16},{40,56},{48,0},{56,40},{64,11... | collective-permute-start | bytes 3932168 | tf_op jit(solution)/shard_map/ppermute | solution.py:135
  86.3 11.4 %collective-permute-start.9 = (bf16[256,5120]{1,0:T(8,128)(2,1)S(1)}, bf16[256,5120]{1,0:T(8,128)(2,1)S(1)}, u32[]{:S(2)}, u32[]{:S(2)}) collective-permute-start(bf16[256,5120]{1,0:T(8,128)(2,1)S(1)} %convolution_convert_fusion), channel_id=1, source_target_pairs={{0,8},{8,0},{1,9},{9,1},{2,10},{10,2},{3,11},{11,3},{4,12},{12,4},... | collective-permute-start | bytes 7864328 | tf_op jit(solution)/shard_map/ppermute | solution.py:322
  118.4 23.5 %collective-permute-start.14 = (bf16[2,4,320,256]{3,2,1,0:T(8,128)(2,1)}, bf16[2,4,320,256]{3,2,1,0:T(8,128)(2,1)S(1)}, u32[]{:S(2)}, u32[]{:S(2)}) collective-permute-start(bf16[2,4,320,256]{3,2,1,0:T(8,128)(2,1)} %get-tuple-element.35), channel_id=1, source_target_pairs={{0,48},{8,24},{16,32},{24,8},{32,16},{40,56},{48,0},{56,40},{64,11... | collective-permute-start | bytes 3932168 | tf_op jit(solution)/shard_map/ppermute | solution.py:135
  119.8 17.1 %collective-permute-start.10 = (bf16[2,4,320,256]{3,2,1,0:T(8,128)(2,1)}, bf16[2,4,320,256]{3,2,1,0:T(8,128)(2,1)}, u32[]{:S(2)}, u32[]{:S(2)}) collective-permute-start(bf16[2,4,320,256]{3,2,1,0:T(8,128)(2,1)} %bitcast.34), channel_id=1, source_target_pairs={{0,192},{8,72},{16,208},{24,88},{32,224},{40,104},{48,240},{56,120... | collective-permute-start | bytes 3932168 | tf_op jit(solution)/shard_map/ppermute | solution.py:135
  129.7 24.6 %all-to-all-start.1 = ((bf16[32,32,512]{2,1,0:T(8,128)(2,1)}), bf16[32,32,512]{2,1,0:T(8,128)(2,1)S(1)}, u32[]{:S(2)}, u32[]{:S(2)}) async-start(bf16[32,32,512]{2,1,0:T(8,128)(2,1)} %bitcast.24), calls=%async_computation.2 | async-start | bytes 2097152 | tf_op jit(solution)/shard_map/all_to_all | solution.py:332
  139.3 19.9 %collective-permute-start.11 = (bf16[4,320,256]{2,1,0:T(8,128)(2,1)}, bf16[4,320,256]{2,1,0:T(8,128)(2,1)}, u32[]{:S(2)}, u32[]{:S(2)}) collective-permute-start(bf16[4,320,256]{2,1,0:T(8,128)(2,1)} %fusion.9), channel_id=1, source_target_pairs={{0,64},{8,200},{16,80},{24,216},{32,96},{40,232},{48,112},{56,248}... | collective-permute-start | bytes 1966088 | tf_op jit(solution)/shard_map/ppermute | solution.py:135
  144.0 18.4 %collective-permute-start.15 = (bf16[4,320,256]{2,1,0:T(8,128)(2,1)}, bf16[4,320,256]{2,1,0:T(8,128)(2,1)}, u32[]{:S(2)}, u32[]{:S(2)}) collective-permute-start(bf16[4,320,256]{2,1,0:T(8,128)(2,1)} %fusion.6), channel_id=1, source_target_pairs={{0,16},{8,56},{16,0},{24,40},{32,48},{40,24},{48,32},{56,8},{64,80... | collective-permute-start | bytes 1966088 | tf_op jit(solution)/shard_map/ppermute | solution.py:135
  160.8 6.5 %collective-permute-start.12 = (bf16[2,320,256]{2,1,0:T(8,128)(2,1)S(1)}, bf16[2,320,256]{2,1,0:T(8,128)(2,1)S(1)}, u32[]{:S(2)}, u32[]{:S(2)}) collective-permute-start(bf16[2,320,256]{2,1,0:T(8,128)(2,1)S(1)} %pad_maximum_fusion.6), channel_id=1, source_target_pairs={{0,48},{8,24},{16,32},{24,8},{32,16},{40,56},{48,0},{56,40},{64,11... | collective-permute-start | bytes 983048 | tf_op jit(solution)/shard_map/ppermute | solution.py:135
  163.8 6.3 %collective-permute-start.16 = (bf16[2,320,256]{2,1,0:T(8,128)(2,1)S(1)}, bf16[2,320,256]{2,1,0:T(8,128)(2,1)S(1)}, u32[]{:S(2)}, u32[]{:S(2)}) collective-permute-start(bf16[2,320,256]{2,1,0:T(8,128)(2,1)S(1)} %pad_maximum_fusion.7), channel_id=1, source_target_pairs={{0,192},{8,72},{16,208},{24,88},{32,224},{40,104},{48,240},{56,120... | collective-permute-start | bytes 983048 | tf_op jit(solution)/shard_map/ppermute | solution.py:135
  167.4 5.5 %collective-permute-start.13 = (bf16[320,256]{1,0:T(8,128)(2,1)S(1)}, bf16[320,256]{1,0:T(8,128)(2,1)S(1)}, u32[]{:S(2)}, u32[]{:S(2)}) collective-permute-start(bf16[320,256]{1,0:T(8,128)(2,1)S(1)} %fusion.29), channel_id=1, source_target_pairs={{0,16},{8,56},{16,0},{24,40},{32,48},{40,24},{48,32},{56,8},{64,80... | collective-permute-start | bytes 491528 | tf_op jit(solution)/shard_map/ppermute | solution.py:135
  170.1 7.0 %collective-permute-start.17 = (bf16[320,256]{1,0:T(8,128)(2,1)S(1)}, bf16[320,256]{1,0:T(8,128)(2,1)S(1)}, u32[]{:S(2)}, u32[]{:S(2)}) collective-permute-start(bf16[320,256]{1,0:T(8,128)(2,1)S(1)} %fusion.30), channel_id=1, source_target_pairs={{0,64},{8,200},{16,80},{24,216},{32,96},{40,232},{48,112},{56,248}... | collective-permute-start | bytes 491528 | tf_op jit(solution)/shard_map/ppermute | solution.py:135
  173.6 6.7 %collective-permute-start.18 = (f32[160,256]{1,0:T(8,128)}, f32[160,256]{1,0:T(8,128)}, u32[]{:S(2)}, u32[]{:S(2)}) collective-permute-start(f32[160,256]{1,0:T(8,128)} %get-tuple-element.63), channel_id=1, source_target_pairs={{0,8},{8,0},{1,9},{9,1},{2,10},{10,2},{3,11},{11,3},{4,12},{12,4},... | collective-permute-start | bytes 491528 | tf_op jit(solution)/shard_map/ppermute | solution.py:356
  (8 other events, 86.1 us)
Sparse Core Ops, SparseCore 0:
  16.3 44.2 reduce-scatter.2
  63.6 46.2 all-gather.1
  118.5 38.4 reduce-scatter.4
